TPU v7x, 256 devices: a whole 4x4x8 slice. The times are simulated.
256 devices in a mesh: region: 32 (over y, z), feat: 8 (over x, core).
Axes of the slice: x: 4, y: 4, z: 8, core: 2. Of those that a mesh axis runs over, the one named last changes fastest.
Arguments:
- enc_feat: bfloat16 [128, 131072], P('feat', 'region'), may hold values from -6 to 6
- send_order: int32 [32, 32], P('region'), may hold values from 0 to 31, each once within a row
- recv_slot: int32 [32, 32], P('region'), may hold values from 0 to 31, each once within a row
- want: int32 [32, 32, 4], P('region'), may hold values from 0 to 15
- neighbours: int32 [1024, 8], P('region'), may hold values from 0 to 159, as said below
- edge_src: int32 [1024, 8, 128], P('region'), may hold values from 0 to 127
- edge_dst: int32 [1024, 8, 128], P('region'), may hold values from 0 to 127
- conductance: bfloat16 [1024, 8, 128], P('region'), may hold values from 0.049804688 to 0.5
- w_in_h: bfloat16 [2, 128, 128], P(None, 'feat'), may hold values from -0.375 to 0.375
- w_in_m: bfloat16 [2, 128, 128], P(None, 'feat'), may hold values from -0.375 to 0.375
- bias_in: float32 [2, 128], P(None, 'feat'), may hold values from -3 to 3
- w_out: bfloat16 [2, 128, 128], P(None, None, 'feat'), may hold values from -0.5 to 0.5
- ln_gain: float32 [2, 128], P(None, 'feat'), may hold values from 0.1 to 1.9
- ln_shift: float32 [2, 128], P(None, 'feat'), may hold values from -2 to 2
- w_read: float32 [128], P('feat'), may hold values from -0.5 to 0.5
Outputs:
- hidden: bfloat16 [128, 131072], P('feat', 'region')
- pressure: float32 [131072], P('region')
Inputs may be any that keep to these rules, and one draw needn't show every extreme that they name: `neighbours`: entry 0 of a block is its own slot within its partition; an entry below 32 is a block of the same partition; an entry 32 + s * 4 + c names panel c that this partition takes from partition s. `send_order`: each row is a permutation of the brick owner's local blocks. `recv_slot`: each row is a permutation of the partition's local slots.
All inputs are finite; a program needn't handle non-finite values.
Results may differ from a plain program's by a relative error of at most 0.0056.
Values may be sent and summed in bfloat16 or wider, within the bound.
A program may use at most 64 MiB of HBM per device.

v0:
```python
import jax
import jax.numpy as jnp
from jax import lax
from jax.sharding import PartitionSpec as P

BLOCK = 128
NBR = 8
EXPORT = 16
CAPACITY = 4
LAYERS = 2


def aggregate(extended, neighbours, edge_src, edge_dst, conductance, share_rows, local_blocks):
    pores = jnp.arange(BLOCK, dtype=jnp.int32)
    message = jnp.zeros((share_rows, local_blocks, BLOCK), jnp.float32)
    for column in range(NBR):
        dst_hot = (edge_dst[:, column, :, None] == pores[None, None, :]).astype(jnp.bfloat16)
        dst_hot = dst_hot * conductance[:, column, :, None]
        src_hot = (edge_src[:, column, :, None] == pores[None, None, :]).astype(jnp.bfloat16)
        tiles = jnp.einsum("bed,bes->bds", dst_hot, src_hot, preferred_element_type=jnp.float32)
        sources = extended[:, neighbours[:, column], :].astype(jnp.float32)
        message = message + jnp.einsum(
            "bds,fbs->fbd", tiles, sources, precision=lax.Precision.HIGHEST
        )
    return message.reshape(share_rows, local_blocks * BLOCK).astype(jnp.bfloat16)


def on_device(
    enc_feat,
    send_order,
    recv_slot,
    want,
    neighbours,
    edge_src,
    edge_dst,
    conductance,
    w_in_h,
    w_in_m,
    bias_in,
    w_out,
    ln_gain,
    ln_shift,
    w_read,
):
    region_count = lax.axis_size("region")
    share_rows = enc_feat.shape[0]
    local_blocks = neighbours.shape[0]
    quota = local_blocks // region_count
    node_count = local_blocks * BLOCK
    bricks = enc_feat.reshape(share_rows, local_blocks, BLOCK)
    outgoing = bricks[:, send_order.reshape(-1), :].reshape(share_rows, region_count, quota, BLOCK)
    incoming = lax.all_to_all(outgoing, "region", split_axis=1, concat_axis=1, tiled=True)
    incoming = incoming.reshape(share_rows, local_blocks, BLOCK)
    state = jnp.zeros_like(incoming).at[:, recv_slot.reshape(-1), :].set(incoming)
    want_here = want.reshape(region_count, CAPACITY)
    lookup = (jnp.arange(region_count, dtype=jnp.int32)[:, None] * EXPORT + want_here).reshape(-1)
    full_in_h, full_in_m, full_bias, full_out, full_gain, full_shift = (
        lax.all_gather(w_in_h.astype(jnp.float32), "feat", axis=1, tiled=True),
        lax.all_gather(w_in_m.astype(jnp.float32), "feat", axis=1, tiled=True),
        lax.all_gather(bias_in, "feat", axis=1, tiled=True),
        lax.all_gather(w_out.astype(jnp.float32), "feat", axis=2, tiled=True),
        lax.all_gather(ln_gain, "feat", axis=1, tiled=True),
        lax.all_gather(ln_shift, "feat", axis=1, tiled=True),
    )
    full_in_h = full_in_h.astype(jnp.bfloat16)
    full_in_m = full_in_m.astype(jnp.bfloat16)
    full_out = full_out.astype(jnp.bfloat16)
    for layer_id in range(LAYERS):
        exports = state[:, local_blocks - EXPORT :, :]
        every = lax.all_gather(exports, "region", axis=1, tiled=True)
        arrived = every[:, lookup, :]
        extended = jnp.concatenate([state, arrived], axis=1)
        message = aggregate(
            extended, neighbours, edge_src, edge_dst, conductance, share_rows, local_blocks
        )
        flat_state = state.reshape(share_rows, node_count)
        stacked = jnp.stack([flat_state, message])
        gathered = lax.all_to_all(stacked, "feat", split_axis=2, concat_axis=1, tiled=True)
        pre = jnp.dot(full_in_h[layer_id], gathered[0], preferred_element_type=jnp.float32)
        pre = pre + jnp.dot(full_in_m[layer_id], gathered[1], preferred_element_type=jnp.float32)
        inner = jnp.maximum(pre + full_bias[layer_id][:, None], 0.0).astype(jnp.bfloat16)
        result = jnp.dot(full_out[layer_id], inner, preferred_element_type=jnp.float32)
        center = jnp.mean(result, axis=0, keepdims=True)
        spread = jnp.mean((result - center) ** 2, axis=0, keepdims=True)
        normed = (result - center) * lax.rsqrt(spread + 1e-05)
        update = normed * full_gain[layer_id][:, None] + full_shift[layer_id][:, None]
        renewed = (gathered[0].astype(jnp.float32) + update).astype(jnp.bfloat16)
        flat_state = lax.all_to_all(renewed, "feat", split_axis=0, concat_axis=1, tiled=True)
        state = flat_state.reshape(share_rows, local_blocks, BLOCK)
    flat_state = state.reshape(share_rows, node_count)
    partial_sum = jnp.sum(w_read[:, None] * flat_state.astype(jnp.float32), axis=0)
    pressure = lax.psum(partial_sum, "feat")
    return (flat_state, pressure)


def solution(mesh):
    return jax.shard_map(
        on_device,
        mesh=mesh,
        in_specs=(
            P("feat", "region"),
            P("region", None),
            P("region", None),
            P("region", None, None),
            P("region", None),
            P("region", None, None),
            P("region", None, None),
            P("region", None, None),
            P(None, "feat", None),
            P(None, "feat", None),
            P(None, "feat"),
            P(None, None, "feat"),
            P(None, "feat"),
            P(None, "feat"),
            P("feat"),
        ),
        out_specs=(P("feat", "region"), P("region")),
        check_vma=False,
    )
```

profile of v0, /device:TPU:1, one launch (start us, length us, event | category | flops | bytes accessed | tf_op | source)
XLA Modules:
  0.0 384.8 jit_solution(11386307244355824578)
XLA Ops:
  7.2 0.7 fusion.95
  8.1 1.2 gather_fusion
  9.3 12.0 %all-to-all-start = ((bf16[16,32,1,128]{3,0,2,1:T(8,128)(2,1)}), bf16[16,32,1,128]{3,0,2,1:T(8,128)(2,1)S(1)}, u32[]{:S(2)}, u32[]{:S(2)}) async-start(bf16[16,32,1,128]{3,0,2,1:T(8,128)(2,1)} %bitcast.6), calls=%async_computation | async-start | bytes 262144 | tf_op jit(solution)/shard_map/all_to_all | solution.py:52
  21.4 1.0 fusion.104
  22.6 0.8 copy.67
  24.7 11.6 %all-gather = f32[8,16,2]{1,2,0:T(2,128)S(1)} all-gather(f32[1,16,2]{1,2,0:T(2,128)} %bitcast.274), channel_id=1, replica_groups=mesh['region'=32,'feat'=8] {'feat'}, dimensions={0}, use_global_device_ids=true | all-gather | bytes 1152 | tf_op jit(solution)/shard_map/all_gather | solution.py:60
  36.4 14.1 %all_gather.25 = bf16[2,128,128]{2,1,0:T(8,128)(2,1)} all-gather(bf16[2,16,128]{2,1,0:T(8,128)(2,1)} %param.23), channel_id=1, replica_groups=mesh['region'=32,'feat'=8] {'feat'}, dimensions={1}, use_global_device_ids=true | all-gather | bytes 73728 | tf_op jit(solution)/shard_map/all_gather | solution.py:58
  51.2 1.5 scatter_fusion
  53.4 14.1 %all_gather.26 = bf16[2,128,128]{2,1,0:T(8,128)(2,1)} all-gather(bf16[2,16,128]{2,1,0:T(8,128)(2,1)} %param.24), channel_id=1, replica_groups=mesh['region'=32,'feat'=8] {'feat'}, dimensions={1}, use_global_device_ids=true | all-gather | bytes 73728 | tf_op jit(solution)/shard_map/all_gather | solution.py:59
  68.0 1.4 fusion.119
  69.6 2.2 fusion.3
  71.8 2.1 fusion.7
  73.9 2.1 fusion.11
  76.0 1.5 fusion.15
  77.5 2.1 fusion.1
  79.6 2.1 fusion.5
  81.7 2.1 fusion.9
  83.8 2.5 fusion.13
  86.4 0.7 stack_reshape.3
  87.1 39.7 %all-gather.6.cloned.1.call-done = bf16[16,512,128]{2,0,1:T(8,128)(2,1)} async-done(((bf16[16,16,128]{2,0,1:T(8,128)(2,1)}), bf16[16,512,128]{2,0,1:T(8,128)(2,1)}) %all-gather.6.cloned.1.call-update) | async-done | bytes 2097168 | tf_op jit(solution)/shard_map/all_gather | solution.py:70
  126.8 2.3 gather_fusion.1
  131.5 1.4 gather_fusion.5
  132.9 1.4 gather_fusion.4
  134.3 1.4 gather_fusion.3
  135.6 0.7 gather_fusion.2
  136.4 3.5 fusion.86
  139.8 2.8 convolution_add_fusion.15
  142.7 1.7 convolution_add_fusion.14
  144.4 1.7 convolution_add_fusion.13
  146.2 1.7 convolution_add_fusion.12
  147.9 1.7 convolution_add_fusion.11
  149.7 1.7 convolution_add_fusion.10
  151.4 1.7 fusion.27
  153.3 3.8 copy.77
  157.2 4.0 %reshape.389 = bf16[8,2,8192]{2,1,0:T(2,128)(2,1)} reshape(bf16[4096,2,16]{2,1,0:T(2,128)(2,1)} %bitcast.235) | data formatting | bytes 524288
  161.2 8.8 %all-to-all-start.1 = ((bf16[8,2,8192]{2,1,0:T(2,128)(2,1)}), bf16[8,2,8192]{2,1,0:T(2,128)(2,1)S(1)}, u32[]{:S(2)}, u32[]{:S(2)}) async-start(bf16[8,2,8192]{2,1,0:T(2,128)(2,1)} %reshape.389), calls=%async_computation.1 | async-start | bytes 524288 | tf_op jit(solution)/shard_map/all_to_all | solution.py:78
  170.0 13.4 %all_gather.28 = bf16[2,128,128]{1,2,0:T(8,128)(2,1)S(1)} all-gather(bf16[2,128,16]{1,2,0:T(8,128)(2,1)S(1)} %copy-done.27), channel_id=1, replica_groups=mesh['region'=32,'feat'=8] {'feat'}, dimensions={2}, use_global_device_ids=true | all-gather | bytes 73728 | tf_op jit(solution)/shard_map/all_gather | solution.py:61
  183.5 10.2 %all-gather.1 = f32[8,16,2]{1,2,0:T(2,128)S(1)} all-gather(f32[1,16,2]{1,2,0:T(2,128)S(1)} %bitcast.275), channel_id=1, replica_groups=mesh['region'=32,'feat'=8] {'feat'}, dimensions={0}, use_global_device_ids=true | all-gather | bytes 1152 | tf_op jit(solution)/shard_map/all_gather | solution.py:62
  193.7 8.1 %all-gather.2 = f32[8,16,2]{1,2,0:T(2,128)S(1)} all-gather(f32[1,16,2]{1,2,0:T(2,128)S(1)} %bitcast.276), channel_id=1, replica_groups=mesh['region'=32,'feat'=8] {'feat'}, dimensions={0}, use_global_device_ids=true | all-gather | bytes 1152 | tf_op jit(solution)/shard_map/all_gather | solution.py:63
  202.5 2.4 reshape.390
  204.9 3.2 copy.94
  209.2 16.7 %all_to_all.70 = bf16[8,16,512]{2,1,0:T(8,128)(2,1)S(1)} all-to-all(bf16[8,16,512]{2,1,0:T(8,128)(2,1)S(1)} %bitcast.250), channel_id=1, replica_groups=mesh['region'=32,'feat'=8] {'feat'}, dimensions={0} | all-to-all | bytes 262144 | tf_op jit(solution)/shard_map/all_to_all | solution.py:88
  226.7 0.7 stack_reshape_reshape.3
  227.5 69.0 %all-gather.8.cloned.1.call-done = bf16[16,512,128]{2,0,1:T(8,128)(2,1)} async-done(((bf16[16,16,128]{2,0,1:T(8,128)(2,1)}), bf16[16,512,128]{2,0,1:T(8,128)(2,1)}) %all-gather.8.cloned.1.call-update) | async-done | bytes 2097168 | tf_op jit(solution)/shard_map/all_gather | solution.py:70
  296.5 2.4 gather_fusion.10
  301.4 1.4 gather_fusion.14
  302.7 1.4 gather_fusion.13
  304.1 1.4 gather_fusion.12
  305.4 0.7 gather_fusion.11
  306.2 3.5 fusion.77
  309.7 2.8 convolution_add_fusion.7
  312.5 1.7 convolution_add_fusion.6
  314.3 1.7 convolution_add_fusion.5
  316.0 1.7 convolution_add_fusion.4
  317.7 1.7 convolution_add_fusion.3
  319.5 1.7 convolution_add_fusion.2
  321.2 1.7 fusion.25
  323.1 2.7 copy.89
  325.9 2.4 reshape.391
  328.3 15.1 %all_to_all.71 = bf16[8,2,8192]{2,1,0:T(2,128)(2,1)S(1)} all-to-all(bf16[8,2,8192]{2,1,0:T(2,128)(2,1)S(1)} %reshape.391), channel_id=1, replica_groups=mesh['region'=32,'feat'=8] {'feat'}, dimensions={0} | all-to-all | bytes 524288 | tf_op jit(solution)/shard_map/all_to_all | solution.py:78
  343.4 1.4 reshape.392
  344.9 1.1 copy.95
  347.0 8.7 %all_to_all.72 = bf16[8,16,512]{2,1,0:T(8,128)(2,1)S(1)} all-to-all(bf16[8,16,512]{2,1,0:T(8,128)(2,1)S(1)} %bitcast.251), channel_id=1, replica_groups=mesh['region'=32,'feat'=8] {'feat'}, dimensions={0} | all-to-all | bytes 262144 | tf_op jit(solution)/shard_map/all_to_all | solution.py:88
  355.9 21.2 %psum.7 = f32[4096]{0:T(1024)} all-reduce(f32[4096]{0:T(1024)S(1)} %bitcast.254), channel_id=1, replica_groups=mesh['region'=32,'feat'=8] {'feat'}, use_global_device_ids=true, to_apply=%region_6.0 | all-reduce | flops 4096 | bytes 32768 | tf_op jit(solution)/shard_map/psum | solution.py:92
  (150 shorter events, 13.6 us)
Async XLA Ops:
  7.2 0.9 copy-start
  7.2 62.2 %copy-start.25 = (s32[32,8,128]{2,1,0:T(8,128)S(1)}, s32[32,8,128]{2,1,0:T(8,128)}, u32[]{:S(2)}) copy-start(s32[32,8,128]{2,1,0:T(8,128)} %param.20) | copy-start | bytes 393220
  7.2 62.3 %copy-start.26 = (s32[32,8,128]{2,1,0:T(8,128)S(1)}, s32[32,8,128]{2,1,0:T(8,128)}, u32[]{:S(2)}) copy-start(s32[32,8,128]{2,1,0:T(8,128)} %param.21) | copy-start | bytes 393220
  9.3 41.8 %all-to-all-start = ((bf16[16,32,1,128]{3,0,2,1:T(8,128)(2,1)}), bf16[16,32,1,128]{3,0,2,1:T(8,128)(2,1)S(1)}, u32[]{:S(2)}, u32[]{:S(2)}) async-start(bf16[16,32,1,128]{3,0,2,1:T(8,128)(2,1)} %bitcast.6), calls=%async_computation | async-start | bytes 262144 | tf_op jit(solution)/shard_map/all_to_all | solution.py:52
  21.4 105.4 %all-gather.6.cloned.1.call-start = ((), (), s32[]{:S(2)}) async-start(), calls=%async_computation.5 | async-start | bytes 2162688 | tf_op jit(solution)/shard_map/all_gather | solution.py:70
  24.7 102.1 %copy-start.28 = (s32[1024]{0:T(1024)}, s32[1024]{0:T(1024)S(1)}, u32[]{:S(2)}) copy-start(s32[1024]{0:T(1024)S(1)} %pad_clamp_fusion.8) | copy-start | bytes 12292
  136.3 3.5 copy-start.5
  136.3 6.3 %copy-start.11 = (f32[32,128,128]{2,1,0:T(8,128)S(1)}, f32[32,128,128]{2,1,0:T(8,128)}, u32[]{:S(2)}) copy-start(f32[32,128,128]{2,1,0:T(8,128)} %fusion.5) | copy-start | bytes 6291460
  136.3 6.3 %copy-start.18 = (bf16[32,16,128]{2,1,0:T(8,128)(2,1)S(1)}, bf16[32,16,128]{2,1,0:T(8,128)(2,1)}, u32[]{:S(2)}) copy-start(bf16[32,16,128]{2,1,0:T(8,128)(2,1)} %gather_fusion.4) | copy-start | bytes 393220
  139.8 4.6 %copy-start.3 = (f32[32,128,128]{2,1,0:T(8,128)S(1)}, f32[32,128,128]{2,1,0:T(8,128)}, u32[]{:S(2)}) copy-start(f32[32,128,128]{2,1,0:T(8,128)} %fusion.7) | copy-start | bytes 6291460
  139.8 4.6 %copy-start.16 = (bf16[32,16,128]{2,1,0:T(8,128)(2,1)S(1)}, bf16[32,16,128]{2,1,0:T(8,128)(2,1)}, u32[]{:S(2)}) copy-start(bf16[32,16,128]{2,1,0:T(8,128)(2,1)} %gather_fusion.5) | copy-start | bytes 393220
  142.7 3.5 copy-start.9
  144.4 3.5 copy-start.1
  146.2 3.5 copy-start.7
  151.4 1.9 copy-start.14
  153.3 16.7 %copy-start.27 = (bf16[2,128,16]{1,2,0:T(8,128)(2,1)S(1)}, bf16[2,128,16]{1,2,0:T(8,128)(2,1)}, u32[]{:S(2)}) copy-start(bf16[2,128,16]{1,2,0:T(8,128)(2,1)} %param.26) | copy-start | bytes 24580
  153.3 30.1 %copy-start.33 = (f32[2,16]{1,0:T(2,128)S(1)}, f32[2,16]{1,0:T(2,128)}, u32[]{:S(2)}) copy-start(f32[2,16]{1,0:T(2,128)} %param.27) | copy-start | bytes 388
  153.3 40.4 %copy-start.34 = (f32[2,16]{1,0:T(2,128)S(1)}, f32[2,16]{1,0:T(2,128)}, u32[]{:S(2)}) copy-start(f32[2,16]{1,0:T(2,128)} %param.28) | copy-start | bytes 388
  161.2 41.3 %all-to-all-start.1 = ((bf16[8,2,8192]{2,1,0:T(2,128)(2,1)}), bf16[8,2,8192]{2,1,0:T(2,128)(2,1)S(1)}, u32[]{:S(2)}, u32[]{:S(2)}) async-start(bf16[8,2,8192]{2,1,0:T(2,128)(2,1)} %reshape.389), calls=%async_computation.1 | async-start | bytes 524288 | tf_op jit(solution)/shard_map/all_to_all | solution.py:78
  170.0 126.5 %all-gather.8.cloned.1.call-start = ((), (), s32[]{:S(2)}) async-start(), calls=%async_computation.6 | async-start | bytes 2162688 | tf_op jit(solution)/shard_map/all_gather | solution.py:70
  183.4 25.1 %copy-start.21 = (bf16[2,128,128]{1,2,0:T(8,128)(2,1)}, bf16[2,128,128]{1,2,0:T(8,128)(2,1)S(1)}, u32[]{:S(2)}) copy-start(bf16[2,128,128]{1,2,0:T(8,128)(2,1)S(1)} %all_gather.28) | copy-start | bytes 196612
  204.9 3.4 copy-start.23
  204.9 3.6 copy-start.19
  204.9 3.6 copy-start.30
  306.2 3.5 copy-start.6
  306.2 6.3 %copy-start.12 = (f32[32,128,128]{2,1,0:T(8,128)S(1)}, f32[32,128,128]{2,1,0:T(8,128)}, u32[]{:S(2)}) copy-start(f32[32,128,128]{2,1,0:T(8,128)} %fusion.5) | copy-start | bytes 6291460
  306.2 6.3 %copy-start.17 = (bf16[32,16,128]{2,1,0:T(8,128)(2,1)S(1)}, bf16[32,16,128]{2,1,0:T(8,128)(2,1)}, u32[]{:S(2)}) copy-start(bf16[32,16,128]{2,1,0:T(8,128)(2,1)} %gather_fusion.13) | copy-start | bytes 393220
  309.7 4.6 %copy-start.4 = (f32[32,128,128]{2,1,0:T(8,128)S(1)}, f32[32,128,128]{2,1,0:T(8,128)}, u32[]{:S(2)}) copy-start(f32[32,128,128]{2,1,0:T(8,128)} %fusion.7) | copy-start | bytes 6291460
  309.7 4.6 %copy-start.15 = (bf16[32,16,128]{2,1,0:T(8,128)(2,1)S(1)}, bf16[32,16,128]{2,1,0:T(8,128)(2,1)}, u32[]{:S(2)}) copy-start(bf16[32,16,128]{2,1,0:T(8,128)(2,1)} %gather_fusion.14) | copy-start | bytes 393220
  312.5 3.5 copy-start.10
  314.2 3.5 copy-start.2
  316.0 3.5 copy-start.8
  321.2 1.9 copy-start.13
  344.8 1.4 copy-start.24
  344.8 1.6 copy-start.20
  344.8 1.6 copy-start.22
  344.8 1.6 copy-start.29
  344.8 2.1 copy-start.31
  344.8 2.1 copy-start.32
  346.0 9.7 %copy-start.35 = (f32[16]{0:T(128)S(1)}, f32[16]{0:T(128)}, u32[]{:S(2)}) copy-start(f32[16]{0:T(128)} %param.29) | copy-start | bytes 196
Sparse Core Ops, SparseCore 0:
  53.5 73.2 all-gather.5
  226.8 69.6 all-gather.7
where the time goes:
time: 392 us; the launch traced here: 385 us
  blocking collectives  133 us (34%)
  waiting for transfers between devices  109 us (28%)
  local copies, waits for them, and re-layouts  51.4 us (13%)
  matrix products  51.3 us (13%)
  starting transfers between devices  20.9 us (5%)
  between operations  15 us (4%)
  other arithmetic  4.26 us (1%)
    all_gather x2, waiting for transfers between devices, on_device(): every = lax.all_gather(exports, 'region', axis=1, tiled=True)  109 us
    dot_general x16, matrix products, aggregate(): jnp.einsum('bds,fbs->fbd', tiles, sources, precision=lax.Precision.HIGHEST)  33.4 us
    all_to_all x2, blocking collectives, on_device(): lax.all_to_all(renewed, 'feat', split_axis=0, concat_axis=1, tiled=True)  25.4 us
    psum x1, blocking collectives, on_device(): pressure = lax.psum(partial_sum, 'feat')  21.2 us
    dot_general x8, matrix products, aggregate(): jnp.einsum('bed,bes->bds', dst_hot, src_hot, preferred_element_type=jnp.f...  16.7 us
    all_to_all x1, blocking collectives, on_device(): lax.all_to_all(stacked, 'feat', split_axis=2, concat_axis=1, tiled=True)  15.1 us
    gather x16, local copies, waits for them, and re-layouts, aggregate(): sources = extended[:, neighbours[:, column], :].astype(jnp.float32)  14.3 us
    all_gather x1, blocking collectives, on_device(): lax.all_gather(w_in_h.astype(jnp.float32), 'feat', axis=1, tiled=True)  14.1 us
  transfers between devices with their start and end apart: 4, of which 2 were waited for; matrix products, arithmetic and copies ran while one was open for 7% of the time, Pallas kernels for 0%

commit v1 on v0

v1 whole, which is shorter than its diff:
```python
import functools

import jax
import jax.numpy as jnp
from jax import lax
from jax.experimental import pallas as pl
from jax.experimental.pallas import tpu as pltpu
from jax.sharding import PartitionSpec as P

BLOCK = 128
NBR = 8
CAPACITY = 4
LAYERS = 2
MESH = pl.DeviceIdType.MESH
NT = (((1,), (1,)), ((), ()))


def wait_bytes(ref, sem):
    pltpu.make_async_copy(ref, ref, sem).wait()


def network_kernel(
    send_order, slot_of, neighbours, want_row, enc_hbm, src_hbm, dst_hbm, cond_hbm,
    w_in_h, w_in_m, w_out, bias_in, ln_gain, ln_shift, w_read,
    hidden, pressure,
    enc, edge_src, edge_dst, cond, enc_stage, enc_in, want_in, want_smem,
    state0, ext0, ext1, halo0, halo1, tiles, message0, message1, x0, x1, renewed,
    exports1, others1, final, press_stage, press_in,
    w_stage, w_all, v_rows, v_stage, v_all, w_out_all,
    local_sem, send_sem, recv_sem,
):
    regions = lax.axis_size("region")
    feats = lax.axis_size("feat")
    me = lax.axis_index("region")
    my_feat = lax.axis_index("feat")
    blocks = neighbours.shape[0]
    exports = blocks // 2
    rows = enc.shape[1]
    width = rows * feats
    half = blocks // feats // 2

    loads_enc = [
        pltpu.make_async_copy(
            enc_hbm.at[:, block * BLOCK : (block + 1) * BLOCK], enc.at[block], local_sem.at[0]
        )
        for block in range(neighbours.shape[0])
    ]
    load_src = pltpu.make_async_copy(src_hbm, edge_src, local_sem.at[1])
    load_dst = pltpu.make_async_copy(dst_hbm, edge_dst, local_sem.at[2])
    load_cond = pltpu.make_async_copy(cond_hbm, cond, local_sem.at[3])
    for load in (*loads_enc, load_src, load_dst, load_cond):
        load.start()

    def region_peer(step):
        return lax.rem(me + step, regions)

    def feat_peer(step):
        return lax.rem(my_feat + step, feats)

    barrier = pltpu.get_barrier_semaphore()

    @pl.loop(1, regions)
    def _(step):
        pl.semaphore_signal(barrier, inc=1, device_id=(region_peer(step), my_feat), device_id_type=MESH)

    @pl.loop(1, feats)
    def _(step):
        pl.semaphore_signal(barrier, inc=1, device_id=(me, feat_peer(step)), device_id_type=MESH)

    eye = (
        lax.broadcasted_iota(jnp.int32, (rows, rows), 0)
        == lax.broadcasted_iota(jnp.int32, (rows, rows), 1)
    )
    mine = pl.ds(pl.multiple_of(my_feat * rows, rows), rows)
    for layer in range(LAYERS):
        w_stage[layer, :, 0:width] = w_in_h[layer]
        w_stage[layer, :, width : 2 * width] = w_in_m[layer]
        w_stage[layer, :, 2 * width :] = lax.dot_general(
            eye.astype(jnp.bfloat16), w_out[layer], NT, preferred_element_type=jnp.float32
        ).astype(jnp.bfloat16)
        w_all[layer, mine, :] = w_stage[layer]
    v_rows[...] = jnp.zeros_like(v_rows)
    v_rows[0:2, :] = bias_in[...]
    v_rows[2:4, :] = ln_gain[...]
    v_rows[4:6, :] = ln_shift[...]
    v_rows[6:7, :] = w_read[...]
    v_stage[...] = jnp.zeros_like(v_stage)
    v_stage[:, 0:8] = lax.dot_general(
        eye.astype(jnp.float32), v_rows[...], NT,
        precision=lax.Precision.HIGHEST, preferred_element_type=jnp.float32,
    )
    v_all[mine, :] = v_stage[...]
    want_in[me] = want_row[...]

    wait_bytes(enc, local_sem.at[0])

    @pl.loop(0, regions)
    def _(step):
        enc_stage[step] = enc[send_order[0, region_peer(step)]]

    enc_in[me] = enc_stage[0]

    pl.semaphore_wait(barrier, regions + feats - 2)

    @pl.loop(1, regions)
    def _(step):
        pltpu.make_async_remote_copy(
            enc_stage.at[step], enc_in.at[me], send_sem.at[0], recv_sem.at[0],
            device_id=(region_peer(step), my_feat), device_id_type=MESH,
        ).start()

    @pl.loop(1, regions)
    def _(step):
        pltpu.make_async_remote_copy(
            want_row, want_in.at[me], send_sem.at[1], recv_sem.at[1],
            device_id=(region_peer(step), my_feat), device_id_type=MESH,
        ).start()

    @pl.loop(1, feats)
    def _(step):
        peer = (me, feat_peer(step))
        pltpu.make_async_remote_copy(
            w_stage, w_all.at[:, mine, :], send_sem.at[2], recv_sem.at[2],
            device_id=peer, device_id_type=MESH,
        ).start()
        pltpu.make_async_remote_copy(
            v_stage, v_all.at[mine, :], send_sem.at[3], recv_sem.at[3],
            device_id=peer, device_id_type=MESH,
        ).start()

    load_src.wait()
    load_dst.wait()
    load_cond.wait()

    def build_tiles(block):
        pores = lax.broadcasted_iota(jnp.int32, (BLOCK, BLOCK), 0)
        for column in range(NBR):
            src = edge_src[block, column : column + 1, :]
            dst = edge_dst[block, column : column + 1, :]
            weight = cond[block, column : column + 1, :].astype(jnp.float32)
            src_hot = jnp.where(pores == src, 1.0, 0.0).astype(jnp.bfloat16)
            dst_hot = jnp.where(pores == dst, weight, 0.0).astype(jnp.bfloat16)
            tiles[block, column * BLOCK : (column + 1) * BLOCK, :] = lax.dot_general(
                src_hot, dst_hot, NT, preferred_element_type=jnp.float32
            ).astype(jnp.bfloat16)

    early = blocks // 4

    @pl.loop(0, early)
    def _(block):
        build_tiles(block)

    wait_bytes(enc_in.at[pl.ds(0, regions - 1)], recv_sem.at[0])

    @pl.loop(0, blocks)
    def _(slot):
        value = enc_in[slot_of[0, slot]]
        state0[slot] = value
        ext0[slot] = value

    wait_bytes(want_in.at[pl.ds(0, regions - 1)], recv_sem.at[1])
    to_smem = pltpu.make_async_copy(want_in, want_smem, local_sem.at[4])
    to_smem.start()
    to_smem.wait()

    def stage_halo(step, source, first, halo):
        region = region_peer(step)
        for panel in range(CAPACITY):
            entry = want_smem[region, 0, me * CAPACITY + panel]
            halo[step, panel] = source[first + entry]

    def send_halo(step, halo, ext, index):
        pltpu.make_async_remote_copy(
            halo.at[step], ext.at[pl.ds(blocks + me * CAPACITY, CAPACITY)],
            send_sem.at[index], recv_sem.at[index],
            device_id=(region_peer(step), my_feat), device_id_type=MESH,
        ).start()

    def exchange_halo(source, first, halo, ext, index):
        @pl.loop(1, regions)
        def _(step):
            stage_halo(step, source, first, halo)
            send_halo(step, halo, ext, index)

        stage_halo(0, source, first, halo)
        for panel in range(CAPACITY):
            ext[blocks + me * CAPACITY + panel] = halo[0, panel]

    exchange_halo(state0, exports, halo0, ext0, 4)

    def share(side):
        def from_peer(step):
            return pl.ds(side * exports + feat_peer(step) * half, half)

        return from_peer

    def to_owner(source, x, side, first_row, index):
        into = pl.ds(pl.multiple_of(first_row + my_feat * rows, rows), rows)
        where = share(side)

        @pl.loop(1, feats)
        def _(step):
            pltpu.make_async_remote_copy(
                source.at[where(step)], x.at[side, :, into, :],
                send_sem.at[index], recv_sem.at[index],
                device_id=(me, feat_peer(step)), device_id_type=MESH,
            ).start()

        x[side, :, into, :] = source[where(0)]

    to_owner(state0, x0, 1, 0, 5)
    to_owner(state0, x0, 0, 0, 6)

    @pl.loop(early, blocks)
    def _(block):
        build_tiles(block)

    wait_bytes(w_all.at[:, pl.ds(0, width - rows), :], recv_sem.at[2])
    wait_bytes(v_all.at[pl.ds(0, width - rows), :], recv_sem.at[3])
    eye_all = (
        lax.broadcasted_iota(jnp.int32, (width, width), 0)
        == lax.broadcasted_iota(jnp.int32, (width, width), 1)
    ).astype(jnp.bfloat16)
    for layer in range(LAYERS):
        w_out_all[layer] = lax.dot_general(
            eye_all, w_all[layer, :, 2 * width :], NT, preferred_element_type=jnp.float32
        ).astype(jnp.bfloat16)

    def aggregate(ext, message, side):
        @pl.loop(side * exports, (side + 1) * exports)
        def _(block):
            sources = jnp.concatenate(
                [ext[neighbours[block, column]] for column in range(NBR)], axis=1
            )
            message[block] = jnp.dot(
                sources, tiles[block], preferred_element_type=jnp.float32
            ).astype(jnp.bfloat16)

    def update(x, side, layer):
        both = jnp.concatenate([x[side, j] for j in range(half)], axis=1)
        vectors = v_all[...]
        pre = jnp.dot(w_all[layer, :, 0 : 2 * width], both, preferred_element_type=jnp.float32)
        inner = jnp.maximum(pre + vectors[:, layer : layer + 1], 0.0).astype(jnp.bfloat16)
        y = jnp.dot(w_out_all[layer], inner, preferred_element_type=jnp.float32)
        mean = jnp.mean(y, axis=0, keepdims=True)
        shifted = y - mean
        var = jnp.mean(shifted * shifted, axis=0, keepdims=True)
        normed = shifted * lax.rsqrt(var + 1e-05)
        change = normed * vectors[:, 2 + layer : 3 + layer] + vectors[:, 4 + layer : 5 + layer]
        return (both[0:width].astype(jnp.float32) + change).astype(jnp.bfloat16)

    def wait_owner(x, side, index):
        wait_bytes(x.at[side, :, pl.ds(0, width - rows), :], recv_sem.at[index])

    def give_back(x, into, side, first, index):
        where = pl.ds(first + my_feat * half, half)

        def part(step):
            return x.at[side, :, pl.ds(pl.multiple_of(feat_peer(step) * rows, rows), rows), :]

        @pl.loop(1, feats)
        def _(step):
            pltpu.make_async_remote_copy(
                part(step), into.at[where], send_sem.at[index], recv_sem.at[index],
                device_id=(me, feat_peer(step)), device_id_type=MESH,
            ).start()

        into[where] = part(0)[...]

    def wait_back(into, index):
        wait_bytes(into.at[pl.ds(0, half * (feats - 1))], recv_sem.at[index])

    halo_bytes = pl.ds(0, (regions - 1) * CAPACITY)
    wait_bytes(ext0.at[halo_bytes], recv_sem.at[4])
    for side in (1, 0):
        aggregate(ext0, message0, side)
        to_owner(message0, x0, side, width, 8 - side)
    for side, into in ((1, exports1), (0, others1)):
        wait_owner(x0, side, 6 - side)
        wait_owner(x0, side, 8 - side)
        new = update(x0, side, 0)
        for j in range(half):
            x1[side, j, 0:width, :] = new[:, j * BLOCK : (j + 1) * BLOCK]
        give_back(x1, into, side, 0, 10 - side)

    wait_back(exports1, 9)
    exchange_halo(exports1, 0, halo1, ext1, 11)
    ext1[pl.ds(exports, exports)] = exports1[...]
    wait_back(others1, 10)
    ext1[pl.ds(0, exports)] = others1[...]
    wait_bytes(ext1.at[halo_bytes], recv_sem.at[11])
    for side in (1, 0):
        aggregate(ext1, message1, side)
        to_owner(message1, x1, side, width, 13 - side)
    for side in (1, 0):
        wait_owner(x1, side, 13 - side)
        new = update(x1, side, 1)
        scaled = v_all[:, 6:7] * new.astype(jnp.float32)
        total = jnp.sum(scaled, axis=0, keepdims=True)
        for j in range(half):
            renewed[side, j] = new[:, j * BLOCK : (j + 1) * BLOCK]
            press_stage[0, side * half + j : side * half + j + 1, :] = (
                total[:, j * BLOCK : (j + 1) * BLOCK]
            )
        give_back(renewed, final, side, side * exports, 15 - side)

    @pl.loop(1, feats)
    def _(step):
        pltpu.make_async_remote_copy(
            press_stage, press_in.at[pl.ds(my_feat, 1)], send_sem.at[16], recv_sem.at[16],
            device_id=(me, feat_peer(step)), device_id_type=MESH,
        ).start()

    press_in[pl.ds(my_feat, 1)] = press_stage[...]
    wait_back(final, 14)
    wait_back(final, 15)
    for block in range(blocks):
        hidden[:, block * BLOCK : (block + 1) * BLOCK] = final[block]
    wait_bytes(press_in.at[pl.ds(0, feats - 1)], recv_sem.at[16])
    for feat in range(feats):
        for side in range(2):
            first = side * exports + feat * half
            pressure[first : first + half, :] = press_in[feat, side * half : (side + 1) * half, :]

    wait_bytes(enc_stage.at[pl.ds(1, regions - 1)], send_sem.at[0])
    wait_bytes(want_in.at[pl.ds(0, regions - 1)], send_sem.at[1])
    wait_bytes(w_all.at[:, pl.ds(0, width - rows), :], send_sem.at[2])
    wait_bytes(v_all.at[pl.ds(0, width - rows), :], send_sem.at[3])
    wait_bytes(halo0.at[pl.ds(1, regions - 1)], send_sem.at[4])
    wait_bytes(halo1.at[pl.ds(1, regions - 1)], send_sem.at[11])
    for index in (5, 6, 7, 8, 9, 10, 12, 13, 14, 15):
        wait_bytes(state0.at[pl.ds(0, half * (feats - 1))], send_sem.at[index])
    wait_bytes(press_in.at[pl.ds(0, feats - 1)], send_sem.at[16])


def on_device(
    enc_feat, send_order, recv_slot, want, neighbours, edge_src, edge_dst, conductance,
    w_in_h, w_in_m, bias_in, w_out, ln_gain, ln_shift, w_read,
):
    regions = lax.axis_size("region")
    feats = lax.axis_size("feat")
    rows, nodes = enc_feat.shape
    blocks = neighbours.shape[0]
    exports = blocks // 2
    width = rows * feats
    own = blocks // feats
    half = own // 2
    panels = regions * CAPACITY
    bf16, f32, i32 = jnp.bfloat16, jnp.float32, jnp.int32
    slots = jnp.arange(blocks, dtype=i32)
    slot_of = jnp.sum(
        jnp.where(recv_slot == slots[:, None], slots[None, :], 0), axis=1, dtype=i32
    ).reshape(1, blocks)
    want_row = jnp.pad(want.reshape(1, panels), ((0, 0), (0, BLOCK - panels)))
    smem = pl.BlockSpec(memory_space=pltpu.SMEM)
    vmem = pl.BlockSpec(memory_space=pltpu.VMEM)
    hbm = pl.BlockSpec(memory_space=pl.ANY)
    phases = 17
    hidden, pressure = pl.pallas_call(
        network_kernel,
        out_shape=(
            jax.ShapeDtypeStruct((rows, nodes), bf16),
            jax.ShapeDtypeStruct((blocks, BLOCK), f32),
        ),
        in_specs=[smem, smem, smem, vmem, hbm, hbm, hbm, hbm] + [vmem] * 7,
        out_specs=(vmem, vmem),
        scratch_shapes=[
            pltpu.VMEM((blocks, rows, BLOCK), bf16),
            pltpu.VMEM((blocks, NBR, BLOCK), i32),
            pltpu.VMEM((blocks, NBR, BLOCK), i32),
            pltpu.VMEM((blocks, NBR, BLOCK), bf16),
            pltpu.VMEM((regions, rows, BLOCK), bf16),
            pltpu.VMEM((regions, rows, BLOCK), bf16),
            pltpu.VMEM((regions, 1, BLOCK), i32),
            pltpu.SMEM((regions, 1, BLOCK), i32),
            pltpu.VMEM((blocks, rows, BLOCK), bf16),
            pltpu.VMEM((blocks + panels, rows, BLOCK), bf16),
            pltpu.VMEM((blocks + panels, rows, BLOCK), bf16),
            pltpu.VMEM((regions, CAPACITY, rows, BLOCK), bf16),
            pltpu.VMEM((regions, CAPACITY, rows, BLOCK), bf16),
            pltpu.VMEM((blocks, NBR * BLOCK, BLOCK), bf16),
            pltpu.VMEM((blocks, rows, BLOCK), bf16),
            pltpu.VMEM((blocks, rows, BLOCK), bf16),
            pltpu.VMEM((2, half, 2 * width, BLOCK), bf16),
            pltpu.VMEM((2, half, 2 * width, BLOCK), bf16),
            pltpu.VMEM((2, half, width, BLOCK), bf16),
            pltpu.VMEM((exports, rows, BLOCK), bf16),
            pltpu.VMEM((exports, rows, BLOCK), bf16),
            pltpu.VMEM((blocks, rows, BLOCK), bf16),
            pltpu.VMEM((1, own, BLOCK), f32),
            pltpu.VMEM((feats, own, BLOCK), f32),
            pltpu.VMEM((LAYERS, rows, 3 * width), bf16),
            pltpu.VMEM((LAYERS, width, 3 * width), bf16),
            pltpu.VMEM((8, rows), f32),
            pltpu.VMEM((rows, BLOCK), f32),
            pltpu.VMEM((width, BLOCK), f32),
            pltpu.VMEM((LAYERS, width, width), bf16),
            pltpu.SemaphoreType.DMA((5,)),
            pltpu.SemaphoreType.DMA((phases,)),
            pltpu.SemaphoreType.DMA((phases,)),
        ],
        compiler_params=pltpu.CompilerParams(
            collective_id=0, has_side_effects=True, vmem_limit_bytes=40 * 1024 * 1024
        ),
        cost_estimate=pl.CostEstimate(
            flops=2 * blocks * NBR * BLOCK * BLOCK * (BLOCK + 2 * rows),
            bytes_accessed=2**20, transcendentals=0,
        ),
    )(
        send_order, slot_of, neighbours, want_row, enc_feat, edge_src, edge_dst, conductance,
        w_in_h, w_in_m, w_out, bias_in, ln_gain, ln_shift, w_read.reshape(1, rows),
    )
    return hidden, pressure.reshape(nodes)


def solution(mesh):
    return jax.shard_map(
        on_device,
        mesh=mesh,
        in_specs=(
            P("feat", "region"),
            P("region", None),
            P("region", None),
            P("region", None, None),
            P("region", None),
            P("region", None, None),
            P("region", None, None),
            P("region", None, None),
            P(None, "feat", None),
            P(None, "feat", None),
            P(None, "feat"),
            P(None, None, "feat"),
            P(None, "feat"),
            P(None, "feat"),
            P("feat"),
        ),
        out_specs=(P("feat", "region"), P("region")),
        check_vma=False,
    )
```

time: 392 us -> 81.2 us (0.21); the launches traced: 385 us -> 80.9 us
  blocking collectives: 133 us -> 0 us
  waiting for transfers between devices: 109 us -> 0 us
  Pallas kernels: 0 us -> 71.5 us
  matrix products: 51.3 us -> 0 us
  local copies, waits for them, and re-layouts: 51.4 us -> 7.83 us
  starting transfers between devices: 20.9 us -> 0 us
  between operations: 15 us -> 0.72 us
    all_gather x2 -> x0, waiting for transfers between devices: 109 us -> none  [on_device(): every = lax.all_gather(exports, 'region', axis=1, tiled=True)]
    pallas_call x0 -> x1, Pallas kernels: none -> 71.5 us  [on_device(): pl.pallas_call(network_kernel, out_shape=(jax.ShapeDtypeStruct((rows, nod...]
    all_gather x6 -> x0, blocking collectives: 71.5 us -> none  [the longest x1 14.1 us: on_device(): lax.all_gather(w_in_h.astype(jnp.float32), 'feat', axis=1, tiled=True)]
    dot_general x28 -> x0, matrix products: 51.3 us -> none  [the longest x16 33.4 us: aggregate(): jnp.einsum('bds,fbs->fbd', tiles, sources, precision=lax.Precision.HIGHEST)]
    all_to_all x3 -> x0, blocking collectives: 40.5 us -> none  [the longest x2 25.4 us: on_device(): lax.all_to_all(renewed, 'feat', split_axis=0, concat_axis=1, tiled=True)]
    psum x1 -> x0, blocking collectives: 21.2 us -> none  [on_device(): pressure = lax.psum(partial_sum, 'feat')]
    all_to_all x2 -> x0, starting transfers between devices: 20.8 us -> none  [the longest x1 12 us: on_device(): lax.all_to_all(outgoing, 'region', split_axis=1, concat_axis=1, tiled=True)]
    gather x19 -> x0, local copies, waits for them, and re-layouts: 20.2 us -> none  [the longest x16 14.3 us: aggregate(): sources = extended[:, neighbours[:, column], :].astype(jnp.float32)]
  transfers between devices with their start and end apart: 4 -> 0, of which waited for: 2 -> 0; matrix products, arithmetic and copies ran while one was open for 7% -> 0% of each run, Pallas kernels for 0% -> 0%
where the time goes in v1:
time: 81.2 us; the launch traced here: 80.9 us
  Pallas kernels  71.5 us (88%)
  local copies, waits for them, and re-layouts  7.83 us (10%)
    pallas_call x1, Pallas kernels, on_device(): pl.pallas_call(network_kernel, out_shape=(jax.ShapeDtypeStruct((rows, nod...  71.5 us
    unnamed x27, local copies, waits for them, and re-layouts  7.72 us

profile of v1, /device:TPU:1, one launch (start us, length us, event | category | flops | bytes accessed | tf_op | source)
XLA Modules:
  0.0 80.9 jit_solution(2409205256793872845)
XLA Ops:
  0.6 0.0 copy-start
  0.6 0.8 select_reduce_fusion
  1.4 0.8 copy.23
  2.2 0.1 reshape.17.want_row
  2.3 0.8 copy.24.neighbours
  3.1 0.0 copy-start.6
  3.1 0.0 copy-start.7
  3.1 0.0 copy-start.8
  3.1 0.0 copy-start.9
  3.1 0.0 copy-start.10
  3.1 0.9 %copy.25.w_out = bf16[2,128,16]{2,1,0:T(8,128)(2,1)S(1)} copy(bf16[2,128,16]{1,2,0:T(8,128)(2,1)} %param.26) | data formatting | bytes 16384 | tf_op args[11]
  4.0 0.0 copy-done
  4.0 0.0 copy-done.6
  4.0 0.0 copy-done.7
  4.0 0.0 copy-done.8
  4.0 0.0 copy-done.9
  4.0 0.0 copy-done.10
  4.0 0.0 copy-start.1
  4.0 0.9 %copy-done.1 = s32[32,8,128]{2,1,0:T(8,128)S(1)} copy-done((s32[32,8,128]{2,1,0:T(8,128)S(1)}, s32[32,8,128]{2,1,0:T(8,128)}, u32[]{:S(2)}) %copy-start.1) | copy-done | bytes 131096
  4.9 0.0 copy-start.2
  4.9 0.9 %copy-done.2 = s32[32,8,128]{2,1,0:T(8,128)S(1)} copy-done((s32[32,8,128]{2,1,0:T(8,128)S(1)}, s32[32,8,128]{2,1,0:T(8,128)}, u32[]{:S(2)}) %copy-start.2) | copy-done | bytes 131096
  5.8 0.0 copy-start.3
  5.8 0.8 %copy-done.3 = bf16[32,8,128]{2,1,0:T(8,128)(2,1)S(1)} copy-done((bf16[32,8,128]{2,1,0:T(8,128)(2,1)S(1)}, bf16[32,8,128]{2,1,0:T(8,128)(2,1)}, u32[]{:S(2)}) %copy-start.3) | copy-done | bytes 65560
  6.7 0.0 copy-start.4
  6.7 0.7 copy-done.4
  7.4 0.0 copy-start.5
  7.4 0.7 copy-done.5
  8.1 71.5 %shard_map.158 = (bf16[16,4096]{1,0:T(8,128)(2,1)S(1)}, f32[32,128]{1,0:T(8,128)S(1)}) custom-call(s32[1,32]{1,0:T(1,128)S(1)} %copy-done.9, s32[1,32]{1,0:T(1,128)S(1)} %bitcast.6, s32[32,8]{1,0:T(8,128)S(1)} %copy.24.neighbours, s32[1,128]{1,0:T(1,128)S(1)} %reshape.17.want_row, bf16[16,4096]{1,0:T(8,128)(2,1)S(1)} %copy-done, ...), custom_call_target="tpu_custom_call" | custom-call | flops 1342177280 | bytes 1048576 | tf_op jit(solution)/shard_map/pallas_call | solution.py:359
  79.6 0.7 copy.28
  80.3 0.6 copy.29
Async XLA Ops:
  0.6 3.4 %copy-start = (bf16[16,4096]{1,0:T(8,128)(2,1)S(1)}, bf16[16,4096]{1,0:T(8,128)(2,1)}, u32[]{:S(2)}) copy-start(bf16[16,4096]{1,0:T(8,128)(2,1)} %enc_hbm.1) | copy-start | bytes 393220
  3.1 0.9 %copy-start.6 = (f32[2,16]{1,0:T(2,128)S(1)}, f32[2,16]{1,0:T(2,128)}, u32[]{:S(2)}) copy-start(f32[2,16]{1,0:T(2,128)} %bias_in.1) | copy-start | bytes 388
  3.1 0.9 %copy-start.7 = (f32[2,16]{1,0:T(2,128)S(1)}, f32[2,16]{1,0:T(2,128)}, u32[]{:S(2)}) copy-start(f32[2,16]{1,0:T(2,128)} %ln_gain.1) | copy-start | bytes 388
  3.1 0.9 %copy-start.8 = (f32[2,16]{1,0:T(2,128)S(1)}, f32[2,16]{1,0:T(2,128)}, u32[]{:S(2)}) copy-start(f32[2,16]{1,0:T(2,128)} %ln_shift.1) | copy-start | bytes 388
  3.1 0.9 %copy-start.9 = (s32[1,32]{1,0:T(1,128)S(1)}, s32[1,32]{1,0:T(1,128)}, u32[]{:S(2)}) copy-start(s32[1,32]{1,0:T(1,128)} %send_order.1) | copy-start | bytes 388
  3.1 0.9 %copy-start.10 = (f32[16]{0:T(128)S(1)}, f32[16]{0:T(128)}, u32[]{:S(2)}) copy-start(f32[16]{0:T(128)} %param.29) | copy-start | bytes 196
  4.0 0.9 %copy-start.1 = (s32[32,8,128]{2,1,0:T(8,128)S(1)}, s32[32,8,128]{2,1,0:T(8,128)}, u32[]{:S(2)}) copy-start(s32[32,8,128]{2,1,0:T(8,128)} %src_hbm.1) | copy-start | bytes 393220
  4.9 0.9 %copy-start.2 = (s32[32,8,128]{2,1,0:T(8,128)S(1)}, s32[32,8,128]{2,1,0:T(8,128)}, u32[]{:S(2)}) copy-start(s32[32,8,128]{2,1,0:T(8,128)} %dst_hbm.1) | copy-start | bytes 393220
  5.8 0.8 %copy-start.3 = (bf16[32,8,128]{2,1,0:T(8,128)(2,1)S(1)}, bf16[32,8,128]{2,1,0:T(8,128)(2,1)}, u32[]{:S(2)}) copy-start(bf16[32,8,128]{2,1,0:T(8,128)(2,1)} %cond_hbm.1) | copy-start | bytes 196612
  6.7 0.7 copy-start.4
  7.4 0.7 copy-start.5

commit v2 on v1

--- a/solution.py
+++ b/solution.py
@@ -20,9 +20,11 @@
 
 
 def network_kernel(
-    send_order, slot_of, neighbours, want_row, enc_hbm, src_hbm, dst_hbm, cond_hbm,
+    order_hbm, slot_hbm, nbr_hbm, want_hbm, enc_hbm, src_hbm, dst_hbm, cond_hbm,
+    w_in_h_hbm, w_in_m_hbm, w_out_hbm, bias_hbm, gain_hbm, shift_hbm, read_hbm,
+    hidden, pressure,
+    send_order, recv_slot, neighbours, want_row, inverse, slot_of,
     w_in_h, w_in_m, w_out, bias_in, ln_gain, ln_shift, w_read,
-    hidden, pressure,
     enc, edge_src, edge_dst, cond, enc_stage, enc_in, want_in, want_smem,
     state0, ext0, ext1, halo0, halo1, tiles, message0, message1, x0, x1, renewed,
     exports1, others1, final, press_stage, press_in,
@@ -33,22 +35,35 @@
     feats = lax.axis_size("feat")
     me = lax.axis_index("region")
     my_feat = lax.axis_index("feat")
-    blocks = neighbours.shape[0]
+    blocks = enc.shape[0]
     exports = blocks // 2
     rows = enc.shape[1]
     width = rows * feats
     half = blocks // feats // 2
 
+    sent = []
+
+    def drain():
+        for ref, index in sent:
+            wait_bytes(ref, send_sem.at[index])
+
     loads_enc = [
         pltpu.make_async_copy(
             enc_hbm.at[:, block * BLOCK : (block + 1) * BLOCK], enc.at[block], local_sem.at[0]
         )
-        for block in range(neighbours.shape[0])
+        for block in range(blocks)
     ]
-    load_src = pltpu.make_async_copy(src_hbm, edge_src, local_sem.at[1])
-    load_dst = pltpu.make_async_copy(dst_hbm, edge_dst, local_sem.at[2])
-    load_cond = pltpu.make_async_copy(cond_hbm, cond, local_sem.at[3])
-    for load in (*loads_enc, load_src, load_dst, load_cond):
+    small = (
+        (order_hbm, send_order), (slot_hbm, recv_slot), (want_hbm, want_row),
+        (w_in_h_hbm, w_in_h), (w_in_m_hbm, w_in_m), (w_out_hbm, w_out), (bias_hbm, bias_in),
+        (gain_hbm, ln_gain), (shift_hbm, ln_shift), (read_hbm, w_read),
+        (src_hbm, edge_src), (dst_hbm, edge_dst), (cond_hbm, cond), (nbr_hbm, neighbours),
+    )
+    loads = [
+        pltpu.make_async_copy(source, target, local_sem.at[1 + at])
+        for at, (source, target) in enumerate(small)
+    ]
+    for load in (*loads[:2], *loads_enc, *loads[2:]):
         load.start()
 
     def region_peer(step):
@@ -67,6 +82,18 @@
     def _(step):
         pl.semaphore_signal(barrier, inc=1, device_id=(me, feat_peer(step)), device_id_type=MESH)
 
+    loads[0].wait()
+    loads[1].wait()
+    wait_bytes(enc, local_sem.at[0])
+
+    @pl.loop(0, regions)
+    def _(step):
+        enc_stage[step] = enc[send_order[0, region_peer(step)]]
+
+    enc_in[me] = enc_stage[0]
+
+    for load in loads[2:10]:
+        load.wait()
     eye = (
         lax.broadcasted_iota(jnp.int32, (rows, rows), 0)
         == lax.broadcasted_iota(jnp.int32, (rows, rows), 1)
@@ -75,9 +102,7 @@
     for layer in range(LAYERS):
         w_stage[layer, :, 0:width] = w_in_h[layer]
         w_stage[layer, :, width : 2 * width] = w_in_m[layer]
-        w_stage[layer, :, 2 * width :] = lax.dot_general(
-            eye.astype(jnp.bfloat16), w_out[layer], NT, preferred_element_type=jnp.float32
-        ).astype(jnp.bfloat16)
+        w_stage[layer, :, 2 * width :] = w_out[layer]
         w_all[layer, mine, :] = w_stage[layer]
     v_rows[...] = jnp.zeros_like(v_rows)
     v_rows[0:2, :] = bias_in[...]
@@ -92,13 +117,13 @@
     v_all[mine, :] = v_stage[...]
     want_in[me] = want_row[...]
 
-    wait_bytes(enc, local_sem.at[0])
-
-    @pl.loop(0, regions)
-    def _(step):
-        enc_stage[step] = enc[send_order[0, region_peer(step)]]
-
-    enc_in[me] = enc_stage[0]
+    slots = lax.broadcasted_iota(jnp.int32, inverse.shape, 1)
+    found = jnp.zeros(inverse.shape, jnp.int32)
+    for source in range(regions):
+        found = jnp.where(slots == recv_slot[0, source], source, found)
+    inverse[...] = found
+    load_slots = pltpu.make_async_copy(inverse, slot_of, local_sem.at[16])
+    load_slots.start()
 
     pl.semaphore_wait(barrier, regions + feats - 2)
 
@@ -128,9 +153,13 @@
             device_id=peer, device_id_type=MESH,
         ).start()
 
-    load_src.wait()
-    load_dst.wait()
-    load_cond.wait()
+    sent.append((enc_stage.at[pl.ds(1, regions - 1)], 0))
+    sent.append((want_in.at[pl.ds(0, regions - 1)], 1))
+    sent.append((w_all.at[:, pl.ds(0, width - rows), :], 2))
+    sent.append((v_all.at[pl.ds(0, width - rows), :], 3))
+
+    for load in loads[10:]:
+        load.wait()
 
     def build_tiles(block):
         pores = lax.broadcasted_iota(jnp.int32, (BLOCK, BLOCK), 0)
@@ -152,6 +181,8 @@
 
     wait_bytes(enc_in.at[pl.ds(0, regions - 1)], recv_sem.at[0])
 
+    load_slots.wait()
+
     @pl.loop(0, blocks)
     def _(slot):
         value = enc_in[slot_of[0, slot]]
@@ -159,14 +190,14 @@
         ext0[slot] = value
 
     wait_bytes(want_in.at[pl.ds(0, regions - 1)], recv_sem.at[1])
-    to_smem = pltpu.make_async_copy(want_in, want_smem, local_sem.at[4])
+    to_smem = pltpu.make_async_copy(want_in, want_smem, local_sem.at[15])
     to_smem.start()
     to_smem.wait()
 
     def stage_halo(step, source, first, halo):
         region = region_peer(step)
         for panel in range(CAPACITY):
-            entry = want_smem[region, 0, me * CAPACITY + panel]
+            entry = want_smem[region, panel, me]
             halo[step, panel] = source[first + entry]
 
     def send_halo(step, halo, ext, index):
@@ -182,6 +213,7 @@
             stage_halo(step, source, first, halo)
             send_halo(step, halo, ext, index)
 
+        sent.append((halo.at[pl.ds(1, regions - 1)], index))
         stage_halo(0, source, first, halo)
         for panel in range(CAPACITY):
             ext[blocks + me * CAPACITY + panel] = halo[0, panel]
@@ -206,6 +238,7 @@
                 device_id=(me, feat_peer(step)), device_id_type=MESH,
             ).start()
 
+        sent.append((state0.at[pl.ds(0, half * (feats - 1))], index))
         x[side, :, into, :] = source[where(0)]
 
     to_owner(state0, x0, 1, 0, 5)
@@ -230,7 +263,7 @@
         @pl.loop(side * exports, (side + 1) * exports)
         def _(block):
             sources = jnp.concatenate(
-                [ext[neighbours[block, column]] for column in range(NBR)], axis=1
+                [ext[neighbours[column, block]] for column in range(NBR)], axis=1
             )
             message[block] = jnp.dot(
                 sources, tiles[block], preferred_element_type=jnp.float32
@@ -265,6 +298,7 @@
                 device_id=(me, feat_peer(step)), device_id_type=MESH,
             ).start()
 
+        sent.append((state0.at[pl.ds(0, half * (feats - 1))], index))
         into[where] = part(0)[...]
 
     def wait_back(into, index):
@@ -311,6 +345,7 @@
             device_id=(me, feat_peer(step)), device_id_type=MESH,
         ).start()
 
+    sent.append((press_in.at[pl.ds(0, feats - 1)], 16))
     press_in[pl.ds(my_feat, 1)] = press_stage[...]
     wait_back(final, 14)
     wait_back(final, 15)
@@ -322,15 +357,7 @@
             first = side * exports + feat * half
             pressure[first : first + half, :] = press_in[feat, side * half : (side + 1) * half, :]
 
-    wait_bytes(enc_stage.at[pl.ds(1, regions - 1)], send_sem.at[0])
-    wait_bytes(want_in.at[pl.ds(0, regions - 1)], send_sem.at[1])
-    wait_bytes(w_all.at[:, pl.ds(0, width - rows), :], send_sem.at[2])
-    wait_bytes(v_all.at[pl.ds(0, width - rows), :], send_sem.at[3])
-    wait_bytes(halo0.at[pl.ds(1, regions - 1)], send_sem.at[4])
-    wait_bytes(halo1.at[pl.ds(1, regions - 1)], send_sem.at[11])
-    for index in (5, 6, 7, 8, 9, 10, 12, 13, 14, 15):
-        wait_bytes(state0.at[pl.ds(0, half * (feats - 1))], send_sem.at[index])
-    wait_bytes(press_in.at[pl.ds(0, feats - 1)], send_sem.at[16])
+    drain()
 
 
 def on_device(
@@ -347,12 +374,6 @@
     half = own // 2
     panels = regions * CAPACITY
     bf16, f32, i32 = jnp.bfloat16, jnp.float32, jnp.int32
-    slots = jnp.arange(blocks, dtype=i32)
-    slot_of = jnp.sum(
-        jnp.where(recv_slot == slots[:, None], slots[None, :], 0), axis=1, dtype=i32
-    ).reshape(1, blocks)
-    want_row = jnp.pad(want.reshape(1, panels), ((0, 0), (0, BLOCK - panels)))
-    smem = pl.BlockSpec(memory_space=pltpu.SMEM)
     vmem = pl.BlockSpec(memory_space=pltpu.VMEM)
     hbm = pl.BlockSpec(memory_space=pl.ANY)
     phases = 17
@@ -362,17 +383,30 @@
             jax.ShapeDtypeStruct((rows, nodes), bf16),
             jax.ShapeDtypeStruct((blocks, BLOCK), f32),
         ),
-        in_specs=[smem, smem, smem, vmem, hbm, hbm, hbm, hbm] + [vmem] * 7,
+        in_specs=[hbm] * 15,
         out_specs=(vmem, vmem),
         scratch_shapes=[
+            pltpu.SMEM((1, blocks), i32),
+            pltpu.SMEM((1, regions), i32),
+            pltpu.SMEM((NBR, blocks), i32),
+            pltpu.VMEM((CAPACITY, regions), i32),
+            pltpu.VMEM((1, BLOCK), i32),
+            pltpu.SMEM((1, BLOCK), i32),
+            pltpu.VMEM((LAYERS, rows, width), bf16),
+            pltpu.VMEM((LAYERS, rows, width), bf16),
+            pltpu.VMEM((LAYERS, rows, width), bf16),
+            pltpu.VMEM((LAYERS, rows), f32),
+            pltpu.VMEM((LAYERS, rows), f32),
+            pltpu.VMEM((LAYERS, rows), f32),
+            pltpu.VMEM((1, rows), f32),
             pltpu.VMEM((blocks, rows, BLOCK), bf16),
             pltpu.VMEM((blocks, NBR, BLOCK), i32),
             pltpu.VMEM((blocks, NBR, BLOCK), i32),
             pltpu.VMEM((blocks, NBR, BLOCK), bf16),
             pltpu.VMEM((regions, rows, BLOCK), bf16),
             pltpu.VMEM((regions, rows, BLOCK), bf16),
-            pltpu.VMEM((regions, 1, BLOCK), i32),
-            pltpu.SMEM((regions, 1, BLOCK), i32),
+            pltpu.VMEM((regions, CAPACITY, regions), i32),
+            pltpu.SMEM((regions, CAPACITY, regions), i32),
             pltpu.VMEM((blocks, rows, BLOCK), bf16),
             pltpu.VMEM((blocks + panels, rows, BLOCK), bf16),
             pltpu.VMEM((blocks + panels, rows, BLOCK), bf16),
@@ -395,20 +429,20 @@
             pltpu.VMEM((rows, BLOCK), f32),
             pltpu.VMEM((width, BLOCK), f32),
             pltpu.VMEM((LAYERS, width, width), bf16),
-            pltpu.SemaphoreType.DMA((5,)),
+            pltpu.SemaphoreType.DMA((17,)),
             pltpu.SemaphoreType.DMA((phases,)),
             pltpu.SemaphoreType.DMA((phases,)),
         ],
         compiler_params=pltpu.CompilerParams(
-            collective_id=0, has_side_effects=True, vmem_limit_bytes=40 * 1024 * 1024
+            collective_id=0, has_side_effects=True, vmem_limit_bytes=60 * 1024 * 1024
         ),
         cost_estimate=pl.CostEstimate(
             flops=2 * blocks * NBR * BLOCK * BLOCK * (BLOCK + 2 * rows),
             bytes_accessed=2**20, transcendentals=0,
         ),
     )(
-        send_order, slot_of, neighbours, want_row, enc_feat, edge_src, edge_dst, conductance,
-        w_in_h, w_in_m, w_out, bias_in, ln_gain, ln_shift, w_read.reshape(1, rows),
+        send_order, recv_slot, neighbours.T, want.reshape(regions, CAPACITY).T, enc_feat,
+        edge_src, edge_dst, conductance, w_in_h, w_in_m, jnp.swapaxes(w_out, 1, 2), bias_in, ln_gain, ln_shift, w_read.reshape(1, rows),
     )
     return hidden, pressure.reshape(nodes)
 

time: 81.2 us -> 75.8 us (0.933)
  local copies, waits for them, and re-layouts: 7.83 us -> 2.18 us
  Pallas kernels: 71.5 us -> 72.8 us
    unnamed x27 -> x4, local copies, waits for them, and re-layouts: 7.72 us -> 2.18 us
    pallas_call x1, Pallas kernels: 71.5 us -> 72.8 us  [on_device(): pl.pallas_call(network_kernel, out_shape=(jax.ShapeDtypeStruct((rows, nod...]
where the time goes in v2:
time: 75.8 us; the launch traced here: 75.7 us
  Pallas kernels  72.8 us (96%)
  local copies, waits for them, and re-layouts  2.18 us (3%)
    pallas_call x1, Pallas kernels, on_device(): pl.pallas_call(network_kernel, out_shape=(jax.ShapeDtypeStruct((rows, nod...  72.8 us
    unnamed x4, local copies, waits for them, and re-layouts  2.18 us

profile of v2, /device:TPU:1, one launch (start us, length us, event | category | flops | bytes accessed | tf_op | source)
XLA Modules:
  0.0 75.7 jit_solution(451639683872993728)
XLA Ops:
  0.6 72.8 %shard_map.158 = (bf16[16,4096]{1,0:T(8,128)(2,1)}, f32[32,128]{1,0:T(8,128)}) custom-call(s32[1,32]{1,0:T(1,128)} %order_hbm.1, s32[1,32]{1,0:T(1,128)} %slot_hbm.1, s32[8,32]{1,0:T(8,128)} %bitcast.9, s32[4,32]{1,0:T(4,128)} %bitcast.10, bf16[16,4096]{1,0:T(8,128)(2,1)} %enc_hbm.1, s32[32,8,128]{2,1,0:T(8,128)} %src_hbm.1, s32[32,8,128]{2,1,0:T(8,128)} %dst_hbm.1, ...), custom_call_target="tpu_custom_call" | custom-call | flops 1342177280 | bytes 1048576 | tf_op jit(solution)/shard_map/pallas_call | solution.py:380
  73.5 0.0 copy-start
  73.5 1.6 %copy.19 = bf16[16,4096]{1,0:T(8,128)(2,1)} copy(bf16[16,4096]{1,0:T(8,128)(2,1)} %get-tuple-element.8) | data formatting | bytes 262144
  75.1 0.0 copy-done
  75.1 0.6 copy.20
Async XLA Ops:
  73.5 1.6 %copy-start = (f32[32,128]{1,0:T(8,128)S(1)}, f32[32,128]{1,0:T(8,128)}, u32[]{:S(2)}) copy-start(f32[32,128]{1,0:T(8,128)} %get-tuple-element.5) | copy-start | bytes 49156

commit v3 on v2

--- a/solution.py
+++ b/solution.py
@@ -23,7 +23,7 @@
     order_hbm, slot_hbm, nbr_hbm, want_hbm, enc_hbm, src_hbm, dst_hbm, cond_hbm,
     w_in_h_hbm, w_in_m_hbm, w_out_hbm, bias_hbm, gain_hbm, shift_hbm, read_hbm,
     hidden, pressure,
-    send_order, recv_slot, neighbours, want_row, inverse, slot_of,
+    send_order, recv_slot, neighbours, want_row, want_out, inverse, slot_of,
     w_in_h, w_in_m, w_out, bias_in, ln_gain, ln_shift, w_read,
     enc, edge_src, edge_dst, cond, enc_stage, enc_in, want_in, want_smem,
     state0, ext0, ext1, halo0, halo1, tiles, message0, message1, x0, x1, renewed,
@@ -115,7 +115,16 @@
         precision=lax.Precision.HIGHEST, preferred_element_type=jnp.float32,
     )
     v_all[mine, :] = v_stage[...]
-    want_in[me] = want_row[...]
+    lanes = lax.broadcasted_iota(jnp.int32, (1, BLOCK), 1)
+
+    @pl.loop(0, regions)
+    def _(region):
+        row = jnp.zeros((1, BLOCK), jnp.int32)
+        for panel in range(CAPACITY):
+            row = jnp.where(lanes == panel, want_row[panel, region], row)
+        want_out[region] = row
+
+    want_in[me] = want_out[me]
 
     slots = lax.broadcasted_iota(jnp.int32, inverse.shape, 1)
     found = jnp.zeros(inverse.shape, jnp.int32)
@@ -137,7 +146,7 @@
     @pl.loop(1, regions)
     def _(step):
         pltpu.make_async_remote_copy(
-            want_row, want_in.at[me], send_sem.at[1], recv_sem.at[1],
+            want_out.at[region_peer(step)], want_in.at[me], send_sem.at[1], recv_sem.at[1],
             device_id=(region_peer(step), my_feat), device_id_type=MESH,
         ).start()
 
@@ -173,9 +182,9 @@
                 src_hot, dst_hot, NT, preferred_element_type=jnp.float32
             ).astype(jnp.bfloat16)
 
-    early = blocks // 4
-
-    @pl.loop(0, early)
+    early = blocks // 8
+
+    @pl.loop(0, early, unroll=min(4, early))
     def _(block):
         build_tiles(block)
 
@@ -197,7 +206,7 @@
     def stage_halo(step, source, first, halo):
         region = region_peer(step)
         for panel in range(CAPACITY):
-            entry = want_smem[region, panel, me]
+            entry = want_smem[region, 0, panel]
             halo[step, panel] = source[first + entry]
 
     def send_halo(step, halo, ext, index):
@@ -244,7 +253,7 @@
     to_owner(state0, x0, 1, 0, 5)
     to_owner(state0, x0, 0, 0, 6)
 
-    @pl.loop(early, blocks)
+    @pl.loop(early, blocks, unroll=min(4, early))
     def _(block):
         build_tiles(block)
 
@@ -260,7 +269,7 @@
         ).astype(jnp.bfloat16)
 
     def aggregate(ext, message, side):
-        @pl.loop(side * exports, (side + 1) * exports)
+        @pl.loop(side * exports, (side + 1) * exports, unroll=min(8, exports))
         def _(block):
             sources = jnp.concatenate(
                 [ext[neighbours[column, block]] for column in range(NBR)], axis=1
@@ -375,7 +384,6 @@
     panels = regions * CAPACITY
     bf16, f32, i32 = jnp.bfloat16, jnp.float32, jnp.int32
     vmem = pl.BlockSpec(memory_space=pltpu.VMEM)
-    hbm = pl.BlockSpec(memory_space=pl.ANY)
     phases = 17
     hidden, pressure = pl.pallas_call(
         network_kernel,
@@ -383,13 +391,14 @@
             jax.ShapeDtypeStruct((rows, nodes), bf16),
             jax.ShapeDtypeStruct((blocks, BLOCK), f32),
         ),
-        in_specs=[hbm] * 15,
+        in_specs=[pl.BlockSpec(memory_space=pltpu.HBM)] * 15,
         out_specs=(vmem, vmem),
         scratch_shapes=[
             pltpu.SMEM((1, blocks), i32),
             pltpu.SMEM((1, regions), i32),
             pltpu.SMEM((NBR, blocks), i32),
-            pltpu.VMEM((CAPACITY, regions), i32),
+            pltpu.SMEM((CAPACITY, regions), i32),
+            pltpu.VMEM((regions, 1, BLOCK), i32),
             pltpu.VMEM((1, BLOCK), i32),
             pltpu.SMEM((1, BLOCK), i32),
             pltpu.VMEM((LAYERS, rows, width), bf16),
@@ -405,8 +414,8 @@
             pltpu.VMEM((blocks, NBR, BLOCK), bf16),
             pltpu.VMEM((regions, rows, BLOCK), bf16),
             pltpu.VMEM((regions, rows, BLOCK), bf16),
-            pltpu.VMEM((regions, CAPACITY, regions), i32),
-            pltpu.SMEM((regions, CAPACITY, regions), i32),
+            pltpu.VMEM((regions, 1, BLOCK), i32),
+            pltpu.SMEM((regions, 1, BLOCK), i32),
             pltpu.VMEM((blocks, rows, BLOCK), bf16),
             pltpu.VMEM((blocks + panels, rows, BLOCK), bf16),
             pltpu.VMEM((blocks + panels, rows, BLOCK), bf16),

time: 75.8 us -> 69.2 us (0.913)
  Pallas kernels: 72.8 us -> 66.2 us
    pallas_call x1, Pallas kernels: 72.8 us -> 66.2 us  [on_device(): pl.pallas_call(network_kernel, out_shape=(jax.ShapeDtypeStruct((rows, nod...]
where the time goes in v3:
time: 69.2 us; the launch traced here: 69 us
  Pallas kernels  66.2 us (96%)
  local copies, waits for them, and re-layouts  2.18 us (3%)
    pallas_call x1, Pallas kernels, on_device(): pl.pallas_call(network_kernel, out_shape=(jax.ShapeDtypeStruct((rows, nod...  66.2 us
    unnamed x4, local copies, waits for them, and re-layouts  2.18 us

profile of v3, /device:TPU:1, one launch (start us, length us, event | category | flops | bytes accessed | tf_op | source)
XLA Modules:
  0.0 69.0 jit_solution(11167349124761482710)
XLA Ops:
  0.6 66.2 %shard_map.158 = (bf16[16,4096]{1,0:T(8,128)(2,1)}, f32[32,128]{1,0:T(8,128)}) custom-call(s32[1,32]{1,0:T(1,128)} %order_hbm.1, s32[1,32]{1,0:T(1,128)} %slot_hbm.1, s32[8,32]{1,0:T(8,128)} %bitcast.9, s32[4,32]{1,0:T(4,128)} %bitcast.10, bf16[16,4096]{1,0:T(8,128)(2,1)} %enc_hbm.1, s32[32,8,128]{2,1,0:T(8,128)} %src_hbm.1, s32[32,8,128]{2,1,0:T(8,128)} %dst_hbm.1, ...), custom_call_target="tpu_custom_call" | custom-call | flops 1342177280 | bytes 1048576 | tf_op jit(solution)/shard_map/pallas_call | solution.py:388
  66.8 0.0 copy-start
  66.8 1.6 %copy.19 = bf16[16,4096]{1,0:T(8,128)(2,1)} copy(bf16[16,4096]{1,0:T(8,128)(2,1)} %get-tuple-element.8) | data formatting | bytes 262144
  68.4 0.0 copy-done
  68.4 0.6 copy.20
Async XLA Ops:
  66.8 1.6 %copy-start = (f32[32,128]{1,0:T(8,128)S(1)}, f32[32,128]{1,0:T(8,128)}, u32[]{:S(2)}) copy-start(f32[32,128]{1,0:T(8,128)} %get-tuple-element.5) | copy-start | bytes 49156

commit v4 on v3

--- a/solution.py
+++ b/solution.py
@@ -28,7 +28,7 @@
     enc, edge_src, edge_dst, cond, enc_stage, enc_in, want_in, want_smem,
     state0, ext0, ext1, halo0, halo1, tiles, message0, message1, x0, x1, renewed,
     exports1, others1, final, press_stage, press_in,
-    w_stage, w_all, v_rows, v_stage, v_all, w_out_all,
+    w_stage, w_all, v_rows, v_stage, v_all, v_wide, w_out_all,
     local_sem, send_sem, recv_sem,
 ):
     regions = lax.axis_size("region")
@@ -63,36 +63,74 @@
         pltpu.make_async_copy(source, target, local_sem.at[1 + at])
         for at, (source, target) in enumerate(small)
     ]
-    for load in (*loads[:2], *loads_enc, *loads[2:]):
+    for load in (loads[0], *loads_enc):
         load.start()
 
+    depth = 8 if regions % 8 == 0 else regions
+    lines = regions // depth
+
+    def apart(order, count):
+        return lax.rem(count + count // 2 + (order + 1) // 2 * (1 - 2 * lax.rem(order, 2)), count)
+
     def region_peer(step):
-        return lax.rem(me + step, regions)
+        line = lax.rem(me // depth + apart(step // depth, lines), lines)
+        return line * depth + lax.rem(me + apart(lax.rem(step, depth), depth), depth)
+
+    itself = regions - 1
 
     def feat_peer(step):
         return lax.rem(my_feat + step, feats)
 
     barrier = pltpu.get_barrier_semaphore()
 
-    @pl.loop(1, regions)
+    @pl.loop(0, itself)
     def _(step):
         pl.semaphore_signal(barrier, inc=1, device_id=(region_peer(step), my_feat), device_id_type=MESH)
 
-    @pl.loop(1, feats)
+    @pl.loop(1, feats, unroll=feats - 1)
     def _(step):
         pl.semaphore_signal(barrier, inc=1, device_id=(me, feat_peer(step)), device_id_type=MESH)
 
+    for load in loads[1:]:
+        load.start()
     loads[0].wait()
-    loads[1].wait()
     wait_bytes(enc, local_sem.at[0])
 
+    @pl.loop(0, regions, unroll=regions)
+    def _(step):
+        enc_stage[step] = enc[send_order[0, region_peer(step)]]
+
+    enc_in[me] = enc_stage[itself]
+
+    pl.semaphore_wait(barrier, regions + feats - 2)
+
+    @pl.loop(0, itself, unroll=itself)
+    def _(step):
+        pltpu.make_async_remote_copy(
+            enc_stage.at[step], enc_in.at[me], send_sem.at[0], recv_sem.at[0],
+            device_id=(region_peer(step), my_feat), device_id_type=MESH,
+        ).start()
+
+    loads[2].wait()
+    lanes = lax.broadcasted_iota(jnp.int32, (1, BLOCK), 1)
+
     @pl.loop(0, regions)
-    def _(step):
-        enc_stage[step] = enc[send_order[0, region_peer(step)]]
-
-    enc_in[me] = enc_stage[0]
-
-    for load in loads[2:10]:
+    def _(region):
+        row = jnp.zeros((1, BLOCK), jnp.int32)
+        for panel in range(CAPACITY):
+            row = jnp.where(lanes == panel, want_row[panel, region], row)
+        want_out[region] = row
+
+    want_in[me] = want_out[me]
+
+    @pl.loop(0, itself, unroll=itself)
+    def _(step):
+        pltpu.make_async_remote_copy(
+            want_out.at[region_peer(step)], want_in.at[me], send_sem.at[1], recv_sem.at[1],
+            device_id=(region_peer(step), my_feat), device_id_type=MESH,
+        ).start()
+
+    for load in loads[3:10]:
         load.wait()
     eye = (
         lax.broadcasted_iota(jnp.int32, (rows, rows), 0)
@@ -115,42 +153,7 @@
         precision=lax.Precision.HIGHEST, preferred_element_type=jnp.float32,
     )
     v_all[mine, :] = v_stage[...]
-    lanes = lax.broadcasted_iota(jnp.int32, (1, BLOCK), 1)
-
-    @pl.loop(0, regions)
-    def _(region):
-        row = jnp.zeros((1, BLOCK), jnp.int32)
-        for panel in range(CAPACITY):
-            row = jnp.where(lanes == panel, want_row[panel, region], row)
-        want_out[region] = row
-
-    want_in[me] = want_out[me]
-
-    slots = lax.broadcasted_iota(jnp.int32, inverse.shape, 1)
-    found = jnp.zeros(inverse.shape, jnp.int32)
-    for source in range(regions):
-        found = jnp.where(slots == recv_slot[0, source], source, found)
-    inverse[...] = found
-    load_slots = pltpu.make_async_copy(inverse, slot_of, local_sem.at[16])
-    load_slots.start()
-
-    pl.semaphore_wait(barrier, regions + feats - 2)
-
-    @pl.loop(1, regions)
-    def _(step):
-        pltpu.make_async_remote_copy(
-            enc_stage.at[step], enc_in.at[me], send_sem.at[0], recv_sem.at[0],
-            device_id=(region_peer(step), my_feat), device_id_type=MESH,
-        ).start()
-
-    @pl.loop(1, regions)
-    def _(step):
-        pltpu.make_async_remote_copy(
-            want_out.at[region_peer(step)], want_in.at[me], send_sem.at[1], recv_sem.at[1],
-            device_id=(region_peer(step), my_feat), device_id_type=MESH,
-        ).start()
-
-    @pl.loop(1, feats)
+    @pl.loop(1, feats, unroll=feats - 1)
     def _(step):
         peer = (me, feat_peer(step))
         pltpu.make_async_remote_copy(
@@ -162,7 +165,16 @@
             device_id=peer, device_id_type=MESH,
         ).start()
 
-    sent.append((enc_stage.at[pl.ds(1, regions - 1)], 0))
+    loads[1].wait()
+    slots = lax.broadcasted_iota(jnp.int32, inverse.shape, 1)
+    found = jnp.zeros(inverse.shape, jnp.int32)
+    for source in range(regions):
+        found = jnp.where(slots == recv_slot[0, source], source, found)
+    inverse[...] = found
+    load_slots = pltpu.make_async_copy(inverse, slot_of, local_sem.at[16])
+    load_slots.start()
+
+    sent.append((enc_stage.at[pl.ds(0, itself)], 0))
     sent.append((want_in.at[pl.ds(0, regions - 1)], 1))
     sent.append((w_all.at[:, pl.ds(0, width - rows), :], 2))
     sent.append((v_all.at[pl.ds(0, width - rows), :], 3))
@@ -192,7 +204,7 @@
 
     load_slots.wait()
 
-    @pl.loop(0, blocks)
+    @pl.loop(0, blocks, unroll=min(8, blocks))
     def _(slot):
         value = enc_in[slot_of[0, slot]]
         state0[slot] = value
@@ -217,15 +229,15 @@
         ).start()
 
     def exchange_halo(source, first, halo, ext, index):
-        @pl.loop(1, regions)
+        @pl.loop(0, itself, unroll=itself)
         def _(step):
             stage_halo(step, source, first, halo)
             send_halo(step, halo, ext, index)
 
-        sent.append((halo.at[pl.ds(1, regions - 1)], index))
-        stage_halo(0, source, first, halo)
+        sent.append((halo.at[pl.ds(0, itself)], index))
+        stage_halo(itself, source, first, halo)
         for panel in range(CAPACITY):
-            ext[blocks + me * CAPACITY + panel] = halo[0, panel]
+            ext[blocks + me * CAPACITY + panel] = halo[itself, panel]
 
     exchange_halo(state0, exports, halo0, ext0, 4)
 
@@ -239,7 +251,7 @@
         into = pl.ds(pl.multiple_of(first_row + my_feat * rows, rows), rows)
         where = share(side)
 
-        @pl.loop(1, feats)
+        @pl.loop(1, feats, unroll=feats - 1)
         def _(step):
             pltpu.make_async_remote_copy(
                 source.at[where(step)], x.at[side, :, into, :],
@@ -268,8 +280,14 @@
             eye_all, w_all[layer, :, 2 * width :], NT, preferred_element_type=jnp.float32
         ).astype(jnp.bfloat16)
 
+    for vector in range(7):
+        v_wide[vector] = jnp.broadcast_to(v_all[:, vector : vector + 1], (width, BLOCK))
+
+    def wide(vector):
+        return jnp.concatenate([v_wide[vector]] * half, axis=1)
+
     def aggregate(ext, message, side):
-        @pl.loop(side * exports, (side + 1) * exports, unroll=min(8, exports))
+        @pl.loop(side * exports, (side + 1) * exports, unroll=min(16, exports))
         def _(block):
             sources = jnp.concatenate(
                 [ext[neighbours[column, block]] for column in range(NBR)], axis=1
@@ -280,15 +298,14 @@
 
     def update(x, side, layer):
         both = jnp.concatenate([x[side, j] for j in range(half)], axis=1)
-        vectors = v_all[...]
         pre = jnp.dot(w_all[layer, :, 0 : 2 * width], both, preferred_element_type=jnp.float32)
-        inner = jnp.maximum(pre + vectors[:, layer : layer + 1], 0.0).astype(jnp.bfloat16)
+        inner = jnp.maximum(pre + wide(layer), 0.0).astype(jnp.bfloat16)
         y = jnp.dot(w_out_all[layer], inner, preferred_element_type=jnp.float32)
         mean = jnp.mean(y, axis=0, keepdims=True)
         shifted = y - mean
         var = jnp.mean(shifted * shifted, axis=0, keepdims=True)
         normed = shifted * lax.rsqrt(var + 1e-05)
-        change = normed * vectors[:, 2 + layer : 3 + layer] + vectors[:, 4 + layer : 5 + layer]
+        change = normed * wide(2 + layer) + wide(4 + layer)
         return (both[0:width].astype(jnp.float32) + change).astype(jnp.bfloat16)
 
     def wait_owner(x, side, index):
@@ -300,7 +317,7 @@
         def part(step):
             return x.at[side, :, pl.ds(pl.multiple_of(feat_peer(step) * rows, rows), rows), :]
 
-        @pl.loop(1, feats)
+        @pl.loop(1, feats, unroll=feats - 1)
         def _(step):
             pltpu.make_async_remote_copy(
                 part(step), into.at[where], send_sem.at[index], recv_sem.at[index],
@@ -338,7 +355,7 @@
     for side in (1, 0):
         wait_owner(x1, side, 13 - side)
         new = update(x1, side, 1)
-        scaled = v_all[:, 6:7] * new.astype(jnp.float32)
+        scaled = wide(6) * new.astype(jnp.float32)
         total = jnp.sum(scaled, axis=0, keepdims=True)
         for j in range(half):
             renewed[side, j] = new[:, j * BLOCK : (j + 1) * BLOCK]
@@ -347,7 +364,7 @@
             )
         give_back(renewed, final, side, side * exports, 15 - side)
 
-    @pl.loop(1, feats)
+    @pl.loop(1, feats, unroll=feats - 1)
     def _(step):
         pltpu.make_async_remote_copy(
             press_stage, press_in.at[pl.ds(my_feat, 1)], send_sem.at[16], recv_sem.at[16],
@@ -437,6 +454,7 @@
             pltpu.VMEM((8, rows), f32),
             pltpu.VMEM((rows, BLOCK), f32),
             pltpu.VMEM((width, BLOCK), f32),
+            pltpu.VMEM((7, width, BLOCK), f32),
             pltpu.VMEM((LAYERS, width, width), bf16),
             pltpu.SemaphoreType.DMA((17,)),
             pltpu.SemaphoreType.DMA((phases,)),

time: 69.2 us -> 68.9 us (level)
  no operation moved by 1% of the time
where the time goes in v4:
time: 68.9 us; the launch traced here: 68.8 us
  Pallas kernels  65.9 us (96%)
  local copies, waits for them, and re-layouts  2.18 us (3%)
    pallas_call x1, Pallas kernels, on_device(): pl.pallas_call(network_kernel, out_shape=(jax.ShapeDtypeStruct((rows, nod...  65.9 us
    unnamed x4, local copies, waits for them, and re-layouts  2.18 us

profile of v4, /device:TPU:1, one launch (start us, length us, event | category | flops | bytes accessed | tf_op | source)
XLA Modules:
  0.0 68.8 jit_solution(7971074297528431686)
XLA Ops:
  0.6 65.9 %shard_map.158 = (bf16[16,4096]{1,0:T(8,128)(2,1)}, f32[32,128]{1,0:T(8,128)}) custom-call(s32[1,32]{1,0:T(1,128)} %order_hbm.1, s32[1,32]{1,0:T(1,128)} %slot_hbm.1, s32[8,32]{1,0:T(8,128)} %bitcast.9, s32[4,32]{1,0:T(4,128)} %bitcast.10, bf16[16,4096]{1,0:T(8,128)(2,1)} %enc_hbm.1, s32[32,8,128]{2,1,0:T(8,128)} %src_hbm.1, s32[32,8,128]{2,1,0:T(8,128)} %dst_hbm.1, ...), custom_call_target="tpu_custom_call" | custom-call | flops 1342177280 | bytes 1048576 | tf_op jit(solution)/shard_map/pallas_call | solution.py:405
  66.6 0.0 copy-start
  66.6 1.6 %copy.19 = bf16[16,4096]{1,0:T(8,128)(2,1)} copy(bf16[16,4096]{1,0:T(8,128)(2,1)} %get-tuple-element.8) | data formatting | bytes 262144
  68.1 0.0 copy-done
  68.2 0.6 copy.20
Async XLA Ops:
  66.6 1.6 %copy-start = (f32[32,128]{1,0:T(8,128)S(1)}, f32[32,128]{1,0:T(8,128)}, u32[]{:S(2)}) copy-start(f32[32,128]{1,0:T(8,128)} %get-tuple-element.5) | copy-start | bytes 49156

commit v5 on v4

--- a/solution.py
+++ b/solution.py
@@ -25,7 +25,7 @@
     hidden, pressure,
     send_order, recv_slot, neighbours, want_row, want_out, inverse, slot_of,
     w_in_h, w_in_m, w_out, bias_in, ln_gain, ln_shift, w_read,
-    enc, edge_src, edge_dst, cond, enc_stage, enc_in, want_in, want_smem,
+    enc, edge_src, edge_dst, cond, enc_stage, enc_in, want_in, want_all, want_smem,
     state0, ext0, ext1, halo0, halo1, tiles, message0, message1, x0, x1, renewed,
     exports1, others1, final, press_stage, press_in,
     w_stage, w_all, v_rows, v_stage, v_all, v_wide, w_out_all,
@@ -63,9 +63,6 @@
         pltpu.make_async_copy(source, target, local_sem.at[1 + at])
         for at, (source, target) in enumerate(small)
     ]
-    for load in (loads[0], *loads_enc):
-        load.start()
-
     depth = 8 if regions % 8 == 0 else regions
     lines = regions // depth
 
@@ -83,7 +80,7 @@
 
     barrier = pltpu.get_barrier_semaphore()
 
-    @pl.loop(0, itself)
+    @pl.loop(0, itself, unroll=itself)
     def _(step):
         pl.semaphore_signal(barrier, inc=1, device_id=(region_peer(step), my_feat), device_id_type=MESH)
 
@@ -91,7 +88,7 @@
     def _(step):
         pl.semaphore_signal(barrier, inc=1, device_id=(me, feat_peer(step)), device_id_type=MESH)
 
-    for load in loads[1:]:
+    for load in (loads[0], loads[2], loads[1], *loads_enc, *loads[3:]):
         load.start()
     loads[0].wait()
     wait_bytes(enc, local_sem.at[0])
@@ -101,6 +98,27 @@
         enc_stage[step] = enc[send_order[0, region_peer(step)]]
 
     enc_in[me] = enc_stage[itself]
+
+    loads[2].wait()
+    lanes = lax.broadcasted_iota(jnp.int32, (1, BLOCK), 1)
+
+    @pl.loop(0, regions)
+    def _(region):
+        row = jnp.zeros((1, BLOCK), jnp.int32)
+        for panel in range(CAPACITY):
+            row = jnp.where(lanes == me * CAPACITY + panel, want_row[panel, region], row)
+        want_out[region] = row
+
+    want_in[me] = want_out[me]
+
+    loads[1].wait()
+    slots = lax.broadcasted_iota(jnp.int32, inverse.shape, 1)
+    found = jnp.zeros(inverse.shape, jnp.int32)
+    for source in range(regions):
+        found = jnp.where(slots == recv_slot[0, source], source, found)
+    inverse[...] = found
+    load_slots = pltpu.make_async_copy(inverse, slot_of, local_sem.at[16])
+    load_slots.start()
 
     pl.semaphore_wait(barrier, regions + feats - 2)
 
@@ -110,18 +128,6 @@
             enc_stage.at[step], enc_in.at[me], send_sem.at[0], recv_sem.at[0],
             device_id=(region_peer(step), my_feat), device_id_type=MESH,
         ).start()
-
-    loads[2].wait()
-    lanes = lax.broadcasted_iota(jnp.int32, (1, BLOCK), 1)
-
-    @pl.loop(0, regions)
-    def _(region):
-        row = jnp.zeros((1, BLOCK), jnp.int32)
-        for panel in range(CAPACITY):
-            row = jnp.where(lanes == panel, want_row[panel, region], row)
-        want_out[region] = row
-
-    want_in[me] = want_out[me]
 
     @pl.loop(0, itself, unroll=itself)
     def _(step):
@@ -165,15 +171,6 @@
             device_id=peer, device_id_type=MESH,
         ).start()
 
-    loads[1].wait()
-    slots = lax.broadcasted_iota(jnp.int32, inverse.shape, 1)
-    found = jnp.zeros(inverse.shape, jnp.int32)
-    for source in range(regions):
-        found = jnp.where(slots == recv_slot[0, source], source, found)
-    inverse[...] = found
-    load_slots = pltpu.make_async_copy(inverse, slot_of, local_sem.at[16])
-    load_slots.start()
-
     sent.append((enc_stage.at[pl.ds(0, itself)], 0))
     sent.append((want_in.at[pl.ds(0, regions - 1)], 1))
     sent.append((w_all.at[:, pl.ds(0, width - rows), :], 2))
@@ -204,21 +201,26 @@
 
     load_slots.wait()
 
-    @pl.loop(0, blocks, unroll=min(8, blocks))
-    def _(slot):
+    def place(slot):
         value = enc_in[slot_of[0, slot]]
         state0[slot] = value
         ext0[slot] = value
 
+    pl.loop(exports, blocks, unroll=exports)(place)
+
     wait_bytes(want_in.at[pl.ds(0, regions - 1)], recv_sem.at[1])
-    to_smem = pltpu.make_async_copy(want_in, want_smem, local_sem.at[15])
+    wants = want_in[0]
+    for region in range(1, regions):
+        wants = wants + want_in[region]
+    want_all[...] = wants
+    to_smem = pltpu.make_async_copy(want_all, want_smem, local_sem.at[15])
     to_smem.start()
     to_smem.wait()
 
     def stage_halo(step, source, first, halo):
         region = region_peer(step)
         for panel in range(CAPACITY):
-            entry = want_smem[region, 0, panel]
+            entry = want_smem[0, region * CAPACITY + panel]
             halo[step, panel] = source[first + entry]
 
     def send_halo(step, halo, ext, index):
@@ -262,6 +264,7 @@
         sent.append((state0.at[pl.ds(0, half * (feats - 1))], index))
         x[side, :, into, :] = source[where(0)]
 
+    pl.loop(0, exports, unroll=exports)(place)
     to_owner(state0, x0, 1, 0, 5)
     to_owner(state0, x0, 0, 0, 6)
 
@@ -432,7 +435,8 @@
             pltpu.VMEM((regions, rows, BLOCK), bf16),
             pltpu.VMEM((regions, rows, BLOCK), bf16),
             pltpu.VMEM((regions, 1, BLOCK), i32),
-            pltpu.SMEM((regions, 1, BLOCK), i32),
+            pltpu.VMEM((1, BLOCK), i32),
+            pltpu.SMEM((1, BLOCK), i32),
             pltpu.VMEM((blocks, rows, BLOCK), bf16),
             pltpu.VMEM((blocks + panels, rows, BLOCK), bf16),
             pltpu.VMEM((blocks + panels, rows, BLOCK), bf16),

time: 68.9 us -> 67.7 us (0.983)
  Pallas kernels: 65.9 us -> 64.7 us
    pallas_call x1, Pallas kernels: 65.9 us -> 64.7 us  [on_device(): pl.pallas_call(network_kernel, out_shape=(jax.ShapeDtypeStruct((rows, nod...]
where the time goes in v5:
time: 67.7 us; the launch traced here: 67.5 us
  Pallas kernels  64.7 us (96%)
  local copies, waits for them, and re-layouts  2.18 us (3%)
    pallas_call x1, Pallas kernels, on_device(): pl.pallas_call(network_kernel, out_shape=(jax.ShapeDtypeStruct((rows, nod...  64.7 us
    unnamed x4, local copies, waits for them, and re-layouts  2.18 us

profile of v5, /device:TPU:1, one launch (start us, length us, event | category | flops | bytes accessed | tf_op | source)
XLA Modules:
  0.0 67.5 jit_solution(17761865552316257239)
XLA Ops:
  0.6 64.7 %shard_map.158 = (bf16[16,4096]{1,0:T(8,128)(2,1)}, f32[32,128]{1,0:T(8,128)}) custom-call(s32[1,32]{1,0:T(1,128)} %order_hbm.1, s32[1,32]{1,0:T(1,128)} %slot_hbm.1, s32[8,32]{1,0:T(8,128)} %bitcast.9, s32[4,32]{1,0:T(4,128)} %bitcast.10, bf16[16,4096]{1,0:T(8,128)(2,1)} %enc_hbm.1, s32[32,8,128]{2,1,0:T(8,128)} %src_hbm.1, s32[32,8,128]{2,1,0:T(8,128)} %dst_hbm.1, ...), custom_call_target="tpu_custom_call" | custom-call | flops 1342177280 | bytes 1048576 | tf_op jit(solution)/shard_map/pallas_call | solution.py:408
  65.3 0.0 copy-start
  65.4 1.6 %copy.19 = bf16[16,4096]{1,0:T(8,128)(2,1)} copy(bf16[16,4096]{1,0:T(8,128)(2,1)} %get-tuple-element.8) | data formatting | bytes 262144
  66.9 0.0 copy-done
  66.9 0.6 copy.20
Async XLA Ops:
  65.3 1.6 %copy-start = (f32[32,128]{1,0:T(8,128)S(1)}, f32[32,128]{1,0:T(8,128)}, u32[]{:S(2)}) copy-start(f32[32,128]{1,0:T(8,128)} %get-tuple-element.5) | copy-start | bytes 49156

commit v6 on v5

--- a/solution.py
+++ b/solution.py
@@ -76,7 +76,9 @@
     itself = regions - 1
 
     def feat_peer(step):
-        return lax.rem(my_feat + step, feats)
+        if isinstance(step, int) and step == 0:
+            return my_feat
+        return lax.rem(my_feat + apart(step - 1, feats), feats)
 
     barrier = pltpu.get_barrier_semaphore()
 

time: 67.7 us -> 67.5 us (level)
  no operation moved by 1% of the time
where the time goes in v6:
time: 67.5 us; the launch traced here: 67.3 us
  Pallas kernels  64.5 us (96%)
  local copies, waits for them, and re-layouts  2.18 us (3%)
    pallas_call x1, Pallas kernels, on_device(): pl.pallas_call(network_kernel, out_shape=(jax.ShapeDtypeStruct((rows, nod...  64.5 us
    unnamed x4, local copies, waits for them, and re-layouts  2.18 us

profile of v6, /device:TPU:1, one launch (start us, length us, event | category | flops | bytes accessed | tf_op | source)
XLA Modules:
  0.0 67.3 jit_solution(12564511750660144300)
XLA Ops:
  0.6 64.5 %shard_map.158 = (bf16[16,4096]{1,0:T(8,128)(2,1)}, f32[32,128]{1,0:T(8,128)}) custom-call(s32[1,32]{1,0:T(1,128)} %order_hbm.1, s32[1,32]{1,0:T(1,128)} %slot_hbm.1, s32[8,32]{1,0:T(8,128)} %bitcast.9, s32[4,32]{1,0:T(4,128)} %bitcast.10, bf16[16,4096]{1,0:T(8,128)(2,1)} %enc_hbm.1, s32[32,8,128]{2,1,0:T(8,128)} %src_hbm.1, s32[32,8,128]{2,1,0:T(8,128)} %dst_hbm.1, ...), custom_call_target="tpu_custom_call" | custom-call | flops 1342177280 | bytes 1048576 | tf_op jit(solution)/shard_map/pallas_call | solution.py:410
  65.1 0.0 copy-start
  65.2 1.6 %copy.19 = bf16[16,4096]{1,0:T(8,128)(2,1)} copy(bf16[16,4096]{1,0:T(8,128)(2,1)} %get-tuple-element.8) | data formatting | bytes 262144
  66.7 0.0 copy-done
  66.7 0.6 copy.20
Async XLA Ops:
  65.1 1.6 %copy-start = (f32[32,128]{1,0:T(8,128)S(1)}, f32[32,128]{1,0:T(8,128)}, u32[]{:S(2)}) copy-start(f32[32,128]{1,0:T(8,128)} %get-tuple-element.5) | copy-start | bytes 49156
